TPU v7x, 32 devices: a whole 2x2x4 slice. The times are simulated.
32 devices in a mesh: group: 4 (over y, x), dev: 8 (over z, core).
Axes of the slice: x: 2, y: 2, z: 4, core: 2. Of those that a mesh axis runs over, the one named last changes fastest.
Arguments:
- species: float32 [6, 64, 32768], P(None, ('group', 'dev')), may hold values from 0.5 to 2
- potential: float32 [64, 32768], P(('group', 'dev')), may hold values from -4 to 4
- pore: int32 [64, 32768], P(('group', 'dev')), may hold values 0 or 1
- openness: float32 [64, 32768], P(('group', 'dev')), may hold values from 0.3 to 1
- neighbours: int32 [64, 6], P(('group', 'dev')), may hold values from 0 to 1
- diffusivity: float32 [6], replicated, may hold values from 0.02 to 0.12
- rate_const: float32 [64], P(('group', 'dev')), may hold values from 0.1 to 1
- opened: int32 [64], P(('group', 'dev')), may hold values 0 or 1
- partner: int32 [32], P(('group', 'dev')), may hold values from 0 to 31, as said below
- give_slot: int32 [32], P(('group', 'dev')), may hold values from 0 to 1
Outputs:
- new_species: float32 [6, 64, 32768], P(None, ('group', 'dev'))
- new_potential: float32 [64, 32768], P(('group', 'dev'))
Inputs may be any that keep to these rules, and one draw needn't show every extreme that they name: partner[partner[q]] = q for every device q; a partner other than q differs from q in exactly one bit of the device index; over all devices at most two distinct bits occur, at most one of them below 8.
All inputs are finite; a program needn't handle non-finite values. No bound on the sum of `pore` or of `opened` on one device may be relied on, other than what follows from the above.
Results may differ from a plain program's by a relative error of at most 0.00002.
Values sent between devices are 32-bit elements; how exact they have to be, the bound alone decides.
No kernel may reach another device: no remote copies, remote signals or barrier semaphores. Data moves between devices by JAX's collectives and lax.ppermute only.
A program may use at most 128 MiB of HBM per device.

v0:
```python
import functools

import jax
import jax.numpy as jnp
from jax import lax
from jax.experimental import pallas as pl
from jax.experimental.pallas import tpu as pltpu
from jax.sharding import PartitionSpec as P


SWEEPS = 8
DEPTH = SWEEPS + 1
LANES = 128

charge_scale = 0.5
screening = 0.5
solubility = 2.0
valences = (2.0, -1.0, 1.0, -1.0, 1.0, 2.0)
reaction_signs = (1.0, 1.0, -1.0, 0.0, 0.0, 0.0)

SIDE = 32
QUADS = 4
YQ = SIDE // QUADS
PAIRS = 3
PLANE = SIDE * YQ
HALF = SIDE // 2

FACE_TBL = DEPTH * SIDE
Y_ROWS = FACE_TBL + 8
EDGE_TBL = 64
EDGE_ROWS = EDGE_TBL + 8
THIRD = 11
ZC_TBL = QUADS * THIRD * YQ
ZC_ROWS = ZC_TBL + 8
ZH_EDGE = 2 * 3 * SIDE
ZH_TBL = ZH_EDGE + 64
ZH_ROWS = ZH_TBL + 32
FIELDS = PAIRS + 1
ION_ROWS = FIELDS * SIDE
X_ROWS = Y_ROWS + ION_ROWS
BLOCKS = SIDE // FIELDS

ZH_PLACE = {
    (n, l): (n, off) if l < 5 else (2, 6 * n + off)
    for n in range(2)
    for l, off in enumerate((0, 8, 15, 21, 26, 0, 3, 5))
}

SIDES = ((-1, 0), (1, 0), (0, -1), (0, 1))
CORNERS = ((-1, -1), (-1, 1), (1, -1), (1, 1))
SPAN = 16
EXT = SIDE + 2 * DEPTH
MIDDLE = 10
PARTS = 3
PART = 4
NEAR = SIDE + 2
PAD = 24


def x_way(s):
    return 0 if s > 0 else 1


def y_way(s):
    return 2 if s > 0 else 3


def z_way(s):
    return 4 if s > 0 else 5


def roll(v, shift):
    shift = shift % LANES
    return v if shift == 0 else pltpu.roll(v, shift, 1)


def lane_of(rows):
    return lax.broadcasted_iota(jnp.int32, (rows, LANES), 1)


def swap_groups(v, lane):
    low = lane < 64
    a0 = jnp.where(low, v[0], roll(v[2], 64))
    a2 = jnp.where(low, roll(v[0], 64), v[2])
    a1 = jnp.where(low, v[1], roll(v[3], 64))
    a3 = jnp.where(low, roll(v[1], 64), v[3])
    even = (lane & 32) == 0
    return (
        jnp.where(even, a0, roll(a1, 32)),
        jnp.where(even, roll(a0, 96), a1),
        jnp.where(even, a2, roll(a3, 32)),
        jnp.where(even, roll(a2, 96), a3),
    )


def sign_rows(neighbours):
    row = lax.broadcasted_iota(jnp.int32, (8, LANES), 0)
    table = jnp.zeros((8, LANES), jnp.float32)
    for way in range(6):
        table = jnp.where(row == way, jnp.where(neighbours[0, way] == 0, 1.0, -1.0), table)
    return table


def pack_kernel(pieces, species_in, potential_in, pore_in, openness_in, neighbours, pd, own, *rest):
    n_out = len(pieces)
    outs, (zlo, zhi) = rest[:n_out], rest[n_out : n_out + 2]
    species, potential, pore, openness, sems = rest[n_out + 2 :]
    parts = []
    for part in range(PARTS):
        copies = []
        for c in range(3):
            x0 = c * THIRD + part * PART
            count = min(PART, (c + 1) * THIRD - x0, SIDE - x0)
            rows = pl.ds(x0 * 16, count * 16)
            for number, (src, dst) in enumerate(
                ((species_in, species), (potential_in, potential), (pore_in, pore), (openness_in, openness))
            ):
                at = (slice(None), rows) if number == 0 else (rows,)
                copies.append(pltpu.make_async_copy(src.at[at], dst.at[at], sems.at[part, c, number]))
                copies[-1].start()
        parts.append(copies)
    where = {name: (outs[k], base) for k, held in enumerate(pieces) for name, base in held}
    lane = lane_of(8)
    lane32 = lane & 31
    low = lane < 64
    table = sign_rows(neighbours)
    own[...] = table

    def planes_of(x):
        d, p = [], []
        for b in range(2):
            rows = pl.ds(x * 16 + b, 8, stride=2)
            total = valences[0] * species[0, rows, :]
            for i in range(1, 2 * PAIRS):
                total = total + valences[i] * species[i, rows, :]
            wet = pore[rows, :].astype(jnp.float32) * openness[rows, :]
            d.append(charge_scale * wet * total)
            p.append(potential[rows, :])
        mixed = []
        for v in swap_groups((p[0], d[0], p[1], d[1]), lane):
            r = roll(v, 64)
            mixed.append(jnp.where(low, v + r, r - v))
        at = pl.ds(pl.multiple_of(x * 8, 8), 8)
        for j in range(QUADS):
            pd[j, at, :] = mixed[j]
        return mixed

    def step(i, blocks=3):
        planes = [planes_of(i + c * THIRD) for c in range(blocks)]
        for j in range(QUADS):
            at = pl.ds(pl.multiple_of((j * THIRD + i) * 8, 8), 8)
            lo = hi = planes[0][j]
            for c in range(1, blocks):
                lo = jnp.where(lane32 >= DEPTH * c, roll(planes[c][j], DEPTH * c), lo)
                hi = jnp.where(lane32 < SIDE - DEPTH * c, roll(planes[c][j], -DEPTH * c), hi)
            zlo[at, :] = lo
            zhi[at, :] = hi

    for part in range(PARTS):
        for c in parts[part]:
            c.wait()
        end = min((part + 1) * PART, THIRD - 1)
        lax.fori_loop(part * PART, end, lambda i, carry: (step(i), carry)[1], 0)
    step(THIRD - 1, 2)

    zlo[ZC_TBL:, :] = table
    zhi[ZC_TBL:, :] = table

    def ion_planes(x, ref, start):
        for k, planes in enumerate(dense_ions(species, pore, openness, x, lane)):
            for j in range(QUADS):
                ref[start + k * SIDE + j * 8 : start + k * SIDE + j * 8 + 8, :] = planes[j]

    for sx, sy in SIDES:
        ref, base = where[(sx, sy)]
        for l in range(DEPTH):
            if sx:
                x = l if sx < 0 else SIDE - 1 - l
                for j in range(QUADS):
                    ref[base + l * SIDE + j * 8 : base + l * SIDE + j * 8 + 8, :] = pd[j, x * 8 : x * 8 + 8, :]
            else:
                y = l if sy < 0 else SIDE - 1 - l
                ref[base + l * SIDE : base + (l + 1) * SIDE, :] = pd[y % 4, pl.ds(y // 4, SIDE, stride=8), :]
        ref[base + FACE_TBL : base + Y_ROWS, :] = table
        if sx:
            ion_planes(0 if sx < 0 else SIDE - 1, ref, base + Y_ROWS)
    for sx, sy in CORNERS:
        ref, base = where[(sx, sy)]
        x0 = 0 if sx < 0 else SIDE - 8
        for m in range(8):
            y = m if sy < 0 else SIDE - 8 + m
            ref[base + m * 8 : base + m * 8 + 8, :] = pd[y % 4, pl.ds(x0 * 8 + y // 4, 8, stride=8), :]
        ref[base + EDGE_TBL : base + EDGE_ROWS, :] = table


def dense_ions(species, pore, openness, x, lane):
    rows = [pl.ds(x * 16 + b, 8, stride=2) for b in range(2)]
    w = [pore[rows[b], :].astype(jnp.float32) * openness[rows[b], :] for b in range(2)]
    s = [[species[n, rows[b], :] for b in range(2)] for n in range(2 * PAIRS)]
    fields = [swap_groups((s[k][0], s[k + PAIRS][0], s[k][1], s[k + PAIRS][1]), lane) for k in range(PAIRS)]
    return fields + [swap_groups((w[0], w[0], w[1], w[1]), lane)]


def ions_kernel(species_in, pore_in, openness_in, sp, wd, ylo, yhi, species, pore, openness, sems):
    parts = []
    for part in range(2):
        rows = pl.ds(part * PLANE, PLANE)
        copies = [
            pltpu.make_async_copy(species_in.at[:, rows], species.at[:, rows], sems.at[part, 0]),
            pltpu.make_async_copy(pore_in.at[rows], pore.at[rows], sems.at[part, 1]),
            pltpu.make_async_copy(openness_in.at[rows], openness.at[rows], sems.at[part, 2]),
        ]
        for c in copies:
            c.start()
        parts.append(copies)
    lane = lane_of(8)

    def step(x, carry):
        at = pl.ds(pl.multiple_of(x * 8, 8), 8)
        for k, planes in enumerate(dense_ions(species, pore, openness, x, lane)):
            for j in range(QUADS):
                if k < PAIRS:
                    sp[k, j, at, :] = planes[j]
                else:
                    wd[j, at, :] = planes[j]
        return carry

    for part in range(2):
        for c in parts[part]:
            c.wait()
        lax.fori_loop(part * HALF, (part + 1) * HALF, step, 0, unroll=2)
    for k in range(FIELDS):
        for y, ref in ((0, ylo), (SIDE - 1, yhi)):
            at = pl.ds(y // 4, SIDE, stride=8)
            ref[k * SIDE : (k + 1) * SIDE, :] = sp[k, y % 4, at, :] if k < PAIRS else wd[y % 4, at, :]


def ion_z_kernel(sp, wd, zlo, zhi):
    lane32 = lane_of(8) & 31

    def step(i, carry):
        for j in range(QUADS):
            lo = hi = jnp.zeros((8, LANES), jnp.float32)
            for spot in range(SIDE):
                block, k = spot // FIELDS, spot % FIELDS
                at = pl.ds(pl.multiple_of((i + block * FIELDS) * 8, 8), 8)
                v = sp[k, j, at, :] if k < PAIRS else wd[j, at, :]
                lo = jnp.where(lane32 == spot, roll(v, spot), lo)
                hi = jnp.where(lane32 == spot, roll(v, spot - 31), hi)
            zat = pl.ds(pl.multiple_of(j * SIDE + i * 8, 8), 8)
            zlo[zat, :] = lo
            zhi[zat, :] = hi
        return carry

    lax.fori_loop(0, FIELDS, step, 0)


def relay_kernel(pieces, *refs):
    arrived, (zl, zh) = refs[:-2], refs[-2:]
    where = {name: (arrived[k], base) for k, held in enumerate(pieces) for name, base in held}
    lane32 = lane_of(SIDE) & 31
    for axis in range(2):
        lo = [jnp.zeros((SIDE, LANES), jnp.float32)] * 3
        hi = [jnp.zeros((SIDE, LANES), jnp.float32)] * 3
        for n in range(2):
            sx, sy = SIDES[2 * axis + n]
            ref, base = where[(-sx, -sy)]
            for l in range(8):
                block, off = ZH_PLACE[n, l]
                width = 8 - l
                v = ref[base + l * SIDE : base + (l + 1) * SIDE, :]
                lo[block] = jnp.where((lane32 >= off) & (lane32 < off + width), roll(v, off), lo[block])
                hi[block] = jnp.where((lane32 <= 31 - off) & (lane32 > 31 - off - width), roll(v, -off), hi[block])
            at = slice(ZH_TBL + (2 * axis + n) * 8, ZH_TBL + (2 * axis + n) * 8 + 8)
            zl[at, :] = ref[base + FACE_TBL : base + Y_ROWS, :]
            zh[at, :] = ref[base + FACE_TBL : base + Y_ROWS, :]
        for block in range(3):
            at = slice((axis * 3 + block) * SIDE, (axis * 3 + block + 1) * SIDE)
            zl[at, :] = lo[block]
            zh[at, :] = hi[block]
    group = lane_of(64) & 31
    lo = jnp.zeros((64, LANES), jnp.float32)
    hi = lo
    for number, (sx, sy) in enumerate(CORNERS):
        ref, base = where[(-sx, -sy)]
        v = ref[base : base + EDGE_TBL, :]
        lo = jnp.where((group >= 8 * number) & (group < 8 * number + 8), roll(v, 8 * number), lo)
        hi = jnp.where((group <= 31 - 8 * number) & (group > 23 - 8 * number), roll(v, -8 * number), hi)
    zl[ZH_EDGE : ZH_EDGE + 64, :] = lo
    zh[ZH_EDGE : ZH_EDGE + 64, :] = hi


def sweep_kernel(pieces, *refs):
    n_in = 10 + len(pieces)
    sources, (sp, wd), scalars = refs[:n_in], refs[n_in : n_in + 2], refs[n_in + 2 : n_in + 6]
    ud, fd, keep, send = refs[n_in + 6 : n_in + 10]
    ua, ub, dn, mx, myp, mym, se_cube, we_cube, zw, udv, fdv, sems, ion_sems, out_sems = refs[n_in + 10 : n_in + 24]
    held = refs[n_in + 24 :]
    copies = [pltpu.make_async_copy(src, dst, sems.at[i]) for i, (src, dst) in enumerate(zip(sources, held))]
    for c in copies:
        c.start()
    late = ion_copies(0, sp, wd, se_cube, we_cube, ion_sems)
    for c in late:
        c.start()
    own, pd, zup, zdn, zhup, zhdn = held[:6]
    yz_halos, arrived = held[6:10], held[10:]
    where = {name: (arrived[k], base) for k, held in enumerate(pieces) for name, base in held}

    lane = lane_of(8)
    lane64 = lane & 63
    low = lane < 64
    core = (lane64 >= 16) & (lane64 < 48)
    upper = lane64 >= 48

    for c in copies:
        c.wait()
    table = {(0, 0): own[...]}
    ztable = {1: {(0, 0): zup[ZC_TBL:, :]}, -1: {(0, 0): zdn[ZC_TBL:, :]}}
    for number, (sx, sy) in enumerate(SIDES):
        ref, base = where[(-sx, -sy)]
        table[(sx, sy)] = ref[base + FACE_TBL : base + Y_ROWS, :]
        for sz, held in ((1, zhup), (-1, zhdn)):
            ztable[sz][(sx, sy)] = held[ZH_TBL + number * 8 : ZH_TBL + number * 8 + 8, :]
    for sx, sy in CORNERS:
        ref, base = where[(-sx, -sy)]
        table[(sx, sy)] = ref[base + EDGE_TBL : base + EDGE_ROWS, :]

    def sign(held, way):
        return jnp.broadcast_to(held[way : way + 1, :], (8, LANES))

    def crossing(way, here, there):
        level = sign(table[here], way)
        beyond = {}
        for sz in (1, -1):
            z = z_way(sz)
            beyond[sz] = sign(ztable[sz][here], way) * sign(table[here], z) * sign(table[there], z)
        m = jnp.where(core, level, jnp.where(upper, beyond[1], beyond[-1]))
        return jnp.where(low, 1.0, m)

    row8 = lax.broadcasted_iota(jnp.int32, (8, LANES), 0)
    one = jnp.ones((8, LANES), jnp.float32)
    for number, sx in enumerate((-1, 1)):
        m = {sy: crossing(x_way(sx), (0, sy), (sx, sy)) for sy in (-1, 0, 1)}
        mx[number, 0:8, :] = jnp.where(row8 < 4, m[-1], m[0])
        mx[number, 8:16, :] = jnp.where(row8 < 4, m[0], m[1])
    y_sign = {}
    for number, sx in enumerate((-1, 0, 1)):
        m = {sy: crossing(y_way(sy), (sx, 0), (sx, sy)) for sy in (-1, 1)}
        y_sign[sx] = m
        myp[number, 0:8, :] = jnp.where(row8 == 3, m[-1], one)
        myp[number, 8:16, :] = jnp.where(row8 == 3, m[1], one)
        mym[number, 0:8, :] = jnp.where(row8 == 4, m[-1], one)
        mym[number, 8:16, :] = jnp.where(row8 == 4, m[1], one)

    outer = {}
    for key, held in table.items():
        m = jnp.where(upper, sign(held, 4), sign(held, 5))
        outer[key] = jnp.where(low, 1.0, m)

    def spread(v, zu, zd, shift_u, shift_d, key):
        rows = v.shape[0]
        tall = lambda a: a if rows == 8 else jnp.concatenate([a] * (rows // 8), axis=0)
        if zu is None:
            return roll(v, 16), roll(v, -16)
        m, c, u = tall(outer[key]), tall(core), tall(upper)
        pot = jnp.where(u, roll(zu, 48 + shift_u), roll(zd, -16 + shift_d)) * m
        rho = jnp.where(u, roll(zu, 16 + shift_u), roll(zd, -48 + shift_d)) * m
        return jnp.where(c, roll(v, 16), pot), jnp.where(c, roll(v, -16), rho)

    def fill(i, c):
        x = i + c * THIRD
        at = pl.ds(pl.multiple_of(x * 8, 8), 8)
        to = pl.ds(pl.multiple_of(PAD + (x + DEPTH) * SPAN + 4, 4), 8)
        for j in range(QUADS):
            zat = pl.ds(pl.multiple_of((j * THIRD + i) * 8, 8), 8)
            pot, rho = spread(pd[j, at, :], zup[zat, :], zdn[zat, :], -DEPTH * c, DEPTH * c, (0, 0))
            ua[j, to, :] = pot
            dn[j, to, :] = rho

    def fill_three(i, carry):
        for c in range(3):
            fill(i, c)
        return carry

    lax.fori_loop(0, THIRD - 1, fill_three, 0)
    fill(THIRD - 1, 0)
    fill(THIRD - 1, 1)

    for number, (sx, sy) in enumerate(SIDES):
        ref, base = where[(-sx, -sy)]
        for l in range(DEPTH):
            v = ref[base + l * SIDE : base + (l + 1) * SIDE, :]
            zu = zd = None
            off = 0
            if l < 8:
                block, off = ZH_PLACE[number % 2, l]
                block += number // 2 * 3
                at = slice(block * SIDE, (block + 1) * SIDE)
                zu, zd = zhup[at, :], zhdn[at, :]
            pot, rho = spread(v, zu, zd, -off, off, (sx, sy))
            if sx:
                x = SIDE + l if sx > 0 else -1 - l
                start = PAD + (x + DEPTH) * SPAN + 4
                for j in range(QUADS):
                    ua[j, start : start + 8, :] = pot[j * 8 : j * 8 + 8]
                    dn[j, start : start + 8, :] = rho[j * 8 : j * 8 + 8]
            else:
                j = l % 4 if sy > 0 else 3 - l % 4
                row = 12 + l // 4 if sy > 0 else 3 - l // 4
                at = pl.ds(PAD + DEPTH * SPAN + row, SIDE, stride=SPAN)
                ua[j, at, :] = pot
                dn[j, at, :] = rho
    for number, (sx, sy) in enumerate(CORNERS):
        ref, base = where[(-sx, -sy)]
        for m in range(8):
            v = ref[base + m * 8 : base + m * 8 + 8, :]
            at = slice(ZH_EDGE + m * 8, ZH_EDGE + m * 8 + 8)
            pot, rho = spread(v, zhup[at, :], zhdn[at, :], -8 * number, 8 * number, (sx, sy))
            row = (12 if sy > 0 else 2) + m // 4
            x = SIDE if sx > 0 else -8
            to = pl.ds(PAD + (x + DEPTH) * SPAN + row, 8, stride=SPAN)
            ua[m % 4, to, :] = pot
            dn[m % 4, to, :] = rho

    scale = 1.0 / (6.0 + screening)

    def slab(src, dst, x, sx, before=None, after=None):
        r = pl.multiple_of(PAD + (x + DEPTH) * SPAN, 8)
        at = pl.ds(r, SPAN)
        c = [src[j, at, :] for j in range(QUADS)]
        for j in range(QUADS):
            left = src[j, pl.ds(r - SPAN, SPAN), :]
            right = src[j, pl.ds(r + SPAN, SPAN), :]
            if before is not None:
                left = left * mx[before]
            if after is not None:
                right = right * mx[after]
            north = c[j + 1] if j < 3 else src[0, pl.ds(r + 1, SPAN), :] * myp[sx + 1]
            south = c[j - 1] if j > 0 else src[3, pl.ds(r - 1, SPAN), :] * mym[sx + 1]
            total = (left + right) + (north + south) + (roll(c[j], 1) + roll(c[j], -1)) + dn[j, at, :]
            dst[j, at, :] = total * scale

    def sweep(src, dst, t):
        def middle(i, carry):
            for n in range(MIDDLE):
                slab(src, dst, 1 + i * MIDDLE + n, 0)
            return carry

        def fringe(i, carry):
            for n in range(2):
                slab(src, dst, -2 - 2 * i - n, -1)
                slab(src, dst, SIDE + 1 + 2 * i + n, 1)
            return carry

        lax.fori_loop(0, (SIDE - 2) // MIDDLE, middle, 0)
        slab(src, dst, -1, -1, after=0)
        slab(src, dst, 0, 0, before=0)
        slab(src, dst, SIDE - 1, 0, after=1)
        slab(src, dst, SIDE, 1, before=1)
        lax.fori_loop(0, (SWEEPS + 1 - t) // 2, fringe, 0)

    def two_sweeps(i, carry):
        sweep(ua, ub, 2 * i + 1)
        sweep(ub, ua, 2 * i + 2)
        return carry

    lax.fori_loop(0, SWEEPS // 2, two_sweeps, 0)

    lane16 = lane_of(SPAN)
    first = (lane16 & 32) == 0
    row16 = lax.broadcasted_iota(jnp.int32, (SPAN, LANES), 0)

    def slots(x, m, centre=False):
        r = pl.multiple_of(PAD + (x + DEPTH) * SPAN, 8)
        near = pl.ds(pl.multiple_of((x + 1) * SPAN, 8), SPAN)
        for j in range(QUADS):
            c = ua[j, pl.ds(r, SPAN), :] * m
            t = roll(c, 64)
            u = 0.5 * jnp.where(lane16 < 64, c + t, t - c)
            if centre:
                udv[j, pl.ds(pl.multiple_of(x * 8, 8), 8), :] = u[4:12]
            fdv[j, near, :] = jnp.where(first, roll(u, -16), roll(u, 16))

    tall = lambda a: jnp.concatenate([a, a], axis=0)
    beside = jnp.where(row16 >= 12, tall(y_sign[0][1]), jnp.where(row16 < 4, tall(y_sign[0][-1]), 1.0))
    slots(-1, mx[0])
    slots(SIDE, mx[1])
    def all_slots(i, carry):
        for n in range(4):
            slots(4 * i + n, beside, True)
        return carry

    lax.fori_loop(0, SIDE // 4, all_slots, 0)
    back = [pltpu.make_async_copy(udv, ud, out_sems.at[0]), pltpu.make_async_copy(fdv, fd, out_sems.at[1])]
    for c in back:
        c.start()
    for c in late:
        c.wait()
    x_halos = [(ref, start + Y_ROWS) for ref, start in (where[(1, 0)], where[(-1, 0)])]
    update_half(0, se_cube, we_cube, zw, own, *x_halos, *yz_halos, udv, fdv, *scalars, keep, send)
    for c in back:
        c.wait()


def ion_copies(half, sp, wd, se_cube, we_cube, sems):
    first, skip = (0, 1) if half == 0 else (half * HALF - 1, 0)
    at, to = pl.ds(first, HALF + 1), (pl.ds(skip, HALF + 1), pl.ds(4, YQ))
    copies = [pltpu.make_async_copy(sp.at[k, :, at], se_cube.at[(k, slice(None), *to)], sems.at[k]) for k in range(PAIRS)]
    copies.append(pltpu.make_async_copy(wd.at[:, at], we_cube.at[(slice(None), *to)], sems.at[PAIRS]))
    return copies


def update_kernel(half, x_starts, sp, wd, *refs):
    sources, scalars, outs = refs[:9], refs[9:13], refs[13:15]
    se_cube, we_cube, zw, sems = refs[15:19]
    held = refs[19:]
    copies = ion_copies(half, sp, wd, se_cube, we_cube, sems)
    copies += [pltpu.make_async_copy(src, dst, sems.at[FIELDS + n]) for n, (src, dst) in enumerate(zip(sources, held))]
    for c in copies:
        c.start()
    for c in copies:
        c.wait()
    own, xdn, xup, *others = held
    update_half(half, se_cube, we_cube, zw, own, (xdn, x_starts[0]), (xup, x_starts[1]), *others, *scalars, *outs)


def update_half(
    half,
    se_cube,
    we_cube,
    zw,
    own,
    xdn,
    xup,
    ydn,
    yup,
    zup,
    zdn,
    ud,
    fd,
    diffusivity,
    rate_const,
    opened,
    give_slot,
    keep,
    send,
):
    x0 = half * HALF
    layers = HALF + 2
    se = se_cube.reshape(PAIRS, QUADS, layers * SPAN, LANES)
    we = we_cube.reshape(QUADS, layers * SPAN, LANES)

    lane = lane_of(8)
    lane32 = lane & 31
    low = lane < 64
    even = (lane & 32) == 0

    def turned(v, way):
        s = jnp.broadcast_to(own[way : way + 1, :], v.shape)
        return jnp.where(s > 0, v, roll(v, 64))

    def put(k, j, rows, v):
        if k < PAIRS:
            se[k, j, rows, :] = v
        else:
            we[j, rows, :] = v

    for k in range(FIELDS):
        (ref, start), way, layer = (xdn, 1, 0) if half == 0 else (xup, 0, layers - 1)
        v = turned(ref[start + k * SIDE : start + (k + 1) * SIDE, :], way)
        for j in range(QUADS):
            put(k, j, slice(layer * SPAN + 4, layer * SPAN + 12), v[j * 8 : j * 8 + 8])
        rows = slice(k * SIDE + x0, k * SIDE + x0 + HALF)
        put(k, 0, pl.ds(SPAN + 12, HALF, stride=SPAN), turned(yup[rows, :], 2))
        put(k, 3, pl.ds(SPAN + 3, HALF, stride=SPAN), turned(ydn[rows, :], 3))

    odd = (lane & 1) == 1
    for j in range(QUADS):
        for i in range(FIELDS):
            rows = slice(j * SIDE + i * 8, j * SIDE + i * 8 + 8)
            zu = turned(zup[rows, :], 4)
            zd = roll(turned(zdn[rows, :], 5), -31)
            both = (jnp.where(odd, zd, zu), jnp.where(odd, zu, zd))
            for c in range(BLOCKS // 2):
                spots = (c + half * (BLOCKS // 2)) * FIELDS
                x = c * FIELDS + i
                for k in range(FIELDS):
                    zw[k, j, x * 8 : x * 8 + 8, :] = roll(both[(spots + k) % 2], 31 - spots - k)

    def by_ion(values, k):
        return jnp.where(even, values[k], values[k + PAIRS])

    half_charge = [by_ion([0.5 * v for v in valences], k) for k in range(PAIRS)]
    rates = [by_ion([diffusivity[i] for i in range(2 * PAIRS)], k) for k in range(PAIRS)]
    signs = [by_ion(reaction_signs, k) for k in range(PAIRS)]
    reactivity = [rate_const[b] * opened[b].astype(jnp.float32) for b in range(2)]
    reactivity = jnp.where(low, reactivity[0], reactivity[1])
    given = give_slot[0]
    top, bottom = lane32 == 31, lane32 == 0
    add = lambda values: functools.reduce(lambda a, b: a + b, values)

    def update(i, carry):
        x = i + x0
        at = pl.ds(pl.multiple_of(i * 8, 8), 8)
        done = [[None] * QUADS for _ in range(PAIRS + 1)]
        for j in range(QUADS):

            def around(ref, lead, layer):
                q = pl.multiple_of(layer * SPAN, 8)
                here = pl.ds(q + 4, 8)
                return (
                    ref[lead + (j, here)],
                    ref[lead + (j, pl.ds(q + 4 + SPAN, 8))],
                    ref[lead + (j, pl.ds(q + 4 - SPAN, 8))],
                    ref[lead + (j + 1, here)] if j < 3 else ref[lead + (0, pl.ds(q + 5, 8))],
                    ref[lead + (j - 1, here)] if j > 0 else ref[lead + (3, pl.ds(q + 3, 8))],
                )

            def all_around(ref, lead, k):
                c, *near = around(ref, lead, i + 1)
                z = zw[k, j, at, :]
                return c, near + [jnp.where(top, z, roll(c, -1)), jnp.where(bottom, z, roll(c, 1))]

            w, near_w = all_around(we, (), PAIRS)
            u = ud[j, pl.ds(pl.multiple_of(x * 8, 8), 8), :]
            phi, *near_phi = around(fd, (), x + 1)
            near_phi += [jnp.where(even, roll(u, -17), roll(u, 15)), jnp.where(even, roll(u, -15), roll(u, 17))]
            drift = [near_w[d] * (phi - near_phi[d]) for d in range(6)]
            w_total, d_total = add(near_w), add(drift)
            conc = []
            for k in range(PAIRS):
                c, near_c = all_around(se, (k,), k)
                spread_w = add([near_w[d] * near_c[d] for d in range(6)])
                spread_d = add([drift[d] * near_c[d] for d in range(6)])
                outflow = w * ((c * w_total - spread_w) + half_charge[k] * (c * d_total + spread_d))
                conc.append(c)
                done[k][j] = c - rates[k] * outflow
            reaction = conc[2] - conc[0] * conc[1] / solubility
            reaction = jnp.where(w > 0, reactivity * reaction, 0.0)
            for k in range(PAIRS):
                done[k][j] = done[k][j] + signs[k] * reaction
            done[PAIRS][j] = phi
        for k in range(PAIRS + 1):
            native = swap_groups(done[k], lane)
            for f in range(2 if k < PAIRS else 1):
                ion = k + f * PAIRS if k < PAIRS else 2 * PAIRS
                send[ion, at, :] = jnp.where(given == 0, native[f], native[2 + f])
                keep[ion, at, :] = jnp.where(given == 0, native[2 + f], native[f])
        return carry

    lax.fori_loop(0, HALF, update, 0, unroll=2)


def place_kernel(give_slot, *refs):
    keep, received, (new_sp, new_pot) = refs[:2], refs[2:4], refs[4:]
    given = give_slot[0]
    ions = new_sp.shape[0]
    for half in range(2):
        rows = [pl.ds(half * PLANE + slot, PLANE // 2, stride=2) for slot in (given, 1 - given)]
        for i in range(ions):
            new_sp[i, rows[0], :] = received[half][i]
            new_sp[i, rows[1], :] = keep[half][i]
        new_pot[rows[0], :] = received[half][ions]
        new_pot[rows[1], :] = keep[half][ions]


VMEM = pl.BlockSpec(memory_space=pltpu.VMEM)
SMEM = pl.BlockSpec(memory_space=pltpu.SMEM)
ANY = pl.BlockSpec(memory_space=pl.ANY)
HBM = pl.BlockSpec(memory_space=pltpu.HBM)
MIB = 1024 * 1024


def grant(mib):
    return pltpu.CompilerParams(vmem_limit_bytes=mib * MIB)


def f32(*shape):
    return jax.ShapeDtypeStruct(shape, jnp.float32)


def rows_of(field):
    lead = field.shape[:-2]
    bricks, cells = field.shape[-2:]
    split = field.reshape(lead + (bricks, cells // LANES, LANES))
    return jnp.swapaxes(split, -3, -2).reshape(lead + (bricks * cells // LANES, LANES))


def cells_of(rows):
    lead = rows.shape[:-2]
    count, lanes = rows.shape[-2:]
    split = rows.reshape(lead + (count // 2, 2, lanes))
    return jnp.swapaxes(split, -3, -2).reshape(lead + (2, count // 2 * lanes))


def moved(block, axis, offset):
    n = lax.axis_size(axis)
    return lax.ppermute(block, axis, [(i, (i + offset) % n) for i in range(n)])


def local(
    species,
    potential,
    pore,
    openness,
    neighbours,
    diffusivity,
    rate_const,
    opened,
    partner,
    give_slot,
):
    ion_count, brick_count, cells = species.shape
    dev_count = lax.axis_size("dev")
    stride = dev_count // 4

    held = {}
    for sx, sy in SIDES + CORNERS:
        offset = (sx + sy * stride) % dev_count
        offset = offset if offset <= dev_count // 2 else offset - dev_count
        rows, pieces = held.get(offset, (0, ()))
        held[offset] = (rows + (X_ROWS if sy == 0 else Y_ROWS if sx == 0 else EDGE_ROWS), pieces + (((sx, sy), rows),))
    offsets = sorted(held, key=lambda o: (-held[o][0], -abs(o), o))
    pieces = tuple(held[o][1] for o in offsets)

    with_face = [k for k, o in enumerate(offsets) if held[o][0] >= Y_ROWS]
    alone = [k for k in range(len(offsets)) if k not in with_face]
    rows = brick_count * PLANE
    species_rows, pore_rows, openness_rows = rows_of(species), rows_of(pore), rows_of(openness)
    field = pltpu.VMEM((rows, LANES), jnp.float32)
    field_int = pltpu.VMEM((rows, LANES), jnp.int32)
    fields = pltpu.VMEM((ion_count, rows, LANES), jnp.float32)
    pd, own, *blocks, down, up = pl.pallas_call(
        functools.partial(pack_kernel, pieces),
        out_shape=(
            f32(QUADS, PLANE, LANES),
            f32(8, LANES),
            *(f32(held[o][0], LANES) for o in offsets),
            f32(ZC_ROWS, LANES),
            f32(ZC_ROWS, LANES),
        ),
        in_specs=[HBM] * 4 + [SMEM],
        out_specs=tuple([VMEM] * (4 + len(offsets))),
        scratch_shapes=[fields, field, field_int, field, pltpu.SemaphoreType.DMA((PARTS, 3, 4))],
        compiler_params=grant(60),
        name="pack",
    )(species_rows, rows_of(potential), pore_rows, openness_rows, neighbours)
    faces = [k for k, o in enumerate(offsets) if held[o][0] >= Y_ROWS]
    rest = faces[-1:] + [k for k in range(len(offsets)) if k not in faces]
    zup = moved(down, "group", -1)
    zdn = moved(up, "group", 1)
    arrived = {k: moved(blocks[k], "dev", offsets[k]) for k in faces[:-1]}

    sp, wd, ydown, yup = pl.pallas_call(
        ions_kernel,
        out_shape=(f32(PAIRS, QUADS, PLANE, LANES), f32(QUADS, PLANE, LANES), *([f32(ION_ROWS, LANES)] * 2)),
        in_specs=[HBM] * 3,
        out_specs=(VMEM,) * 4,
        scratch_shapes=[fields, field_int, field, pltpu.SemaphoreType.DMA((2, 3))],
        compiler_params=grant(60),
        name="ions",
    )(species_rows, pore_rows, openness_rows)

    zup, zdn, sp, wd, *more = lax.optimization_barrier((zup, zdn, sp, wd, *(blocks[k] for k in rest)))
    arrived.update((k, moved(block, "dev", offsets[k])) for k, block in zip(rest, more))

    zdown, zupper = pl.pallas_call(
        ion_z_kernel,
        out_shape=(f32(ION_ROWS, LANES),) * 2,
        in_specs=[VMEM] * 2,
        out_specs=(VMEM,) * 2,
        compiler_params=grant(8),
        name="ion_z_faces",
    )(sp, wd)

    z_halos = [moved(zdown, "group", -1), moved(zupper, "group", 1)]
    arrived = [arrived[k] for k in range(len(offsets))]

    zl, zh = pl.pallas_call(
        functools.partial(relay_kernel, pieces),
        out_shape=(f32(ZH_ROWS, LANES),) * 2,
        in_specs=[VMEM] * len(offsets),
        out_specs=(VMEM, VMEM),
        compiler_params=grant(6),
        name="relay",
    )(*arrived)
    ydown, yup, zl, zh = lax.optimization_barrier((ydown, yup, zl, zh))
    zhup = moved(zl, "group", -1)
    zhdn = moved(zh, "group", 1)
    y_halos = [moved(yup, "dev", stride), moved(ydown, "dev", -stride)]

    wide = pltpu.VMEM((QUADS, EXT * SPAN + 2 * PAD, LANES), jnp.float32)
    by_layer = lambda a: a.reshape(a.shape[:-2] + (SIDE, YQ, LANES))
    sp, wd = by_layer(sp), by_layer(wd)
    scalars = (diffusivity, rate_const, opened, give_slot)
    half_out = (f32(ion_count + 1, PLANE // 2, LANES),) * 2
    half_scratch = [
        pltpu.VMEM((PAIRS, QUADS, HALF + 2, SPAN, LANES), jnp.float32),
        pltpu.VMEM((QUADS, HALF + 2, SPAN, LANES), jnp.float32),
        pltpu.VMEM((FIELDS, QUADS, PLANE // 2, LANES), jnp.float32),
    ]
    sources = (own, pd, zup, zdn, zhup, zhdn, *y_halos, *z_halos, *arrived)
    ud, fd, *first_half = pl.pallas_call(
        functools.partial(sweep_kernel, pieces),
        out_shape=(f32(QUADS, PLANE, LANES), f32(QUADS, NEAR * SPAN, LANES), *half_out),
        in_specs=[HBM] * (len(sources) + 2) + [SMEM] * 4,
        out_specs=(HBM, HBM, VMEM, VMEM),
        scratch_shapes=[
            wide,
            wide,
            wide,
            pltpu.VMEM((2, SPAN, LANES), jnp.float32),
            pltpu.VMEM((3, SPAN, LANES), jnp.float32),
            pltpu.VMEM((3, SPAN, LANES), jnp.float32),
            *half_scratch,
            pltpu.VMEM((QUADS, PLANE, LANES), jnp.float32),
            pltpu.VMEM((QUADS, NEAR * SPAN, LANES), jnp.float32),
            pltpu.SemaphoreType.DMA((len(sources),)),
            pltpu.SemaphoreType.DMA((FIELDS,)),
            pltpu.SemaphoreType.DMA((2,)),
            *(pltpu.VMEM(a.shape, jnp.float32) for a in sources),
        ],
        compiler_params=grant(60),
        name="sweeps",
    )(*sources, sp, wd, *scalars)

    def second_half():
        x_halos, x_starts = [], []
        for sx in (1, -1):
            for k, parts in enumerate(pieces):
                for name, start in parts:
                    if name == (sx, 0):
                        x_halos.append(arrived[k])
                        x_starts.append(start + Y_ROWS)
        sources = (own, *x_halos, *y_halos, *z_halos, ud, fd)
        return pl.pallas_call(
            functools.partial(update_kernel, 1, x_starts),
            out_shape=half_out,
            in_specs=[HBM] * (len(sources) + 2) + [SMEM] * 4,
            out_specs=(VMEM, VMEM),
            scratch_shapes=[
                *half_scratch,
                pltpu.SemaphoreType.DMA((FIELDS + len(sources),)),
                *(pltpu.VMEM(a.shape, jnp.float32) for a in sources),
            ],
            compiler_params=grant(32),
            name="update",
        )(sp, wd, *sources, *scalars)

    def placed(kept, received):
        new_sp, new_pot = pl.pallas_call(
            place_kernel,
            out_shape=(f32(ion_count, rows, LANES), f32(rows, LANES)),
            in_specs=[SMEM] + [VMEM] * 4,
            out_specs=(VMEM, VMEM),
            compiler_params=grant(8),
            name="place",
        )(give_slot, *kept, *received)
        return cells_of(new_sp), cells_of(new_pot)

    def finished(route):
        across = lambda block: block if route is None else lax.ppermute(block, ("group", "dev"), route)
        keep, send = first_half
        keep_more, send_more = second_half()
        return placed((keep, keep_more), (across(send), across(send_more)))

    total = lax.axis_size("group") * dev_count
    own_index = lax.axis_index("group") * dev_count + lax.axis_index("dev")
    apart = jnp.bitwise_xor(own_index, partner[0])
    branch = jnp.int32(0)
    branches = [lambda: finished(None)]
    for bit in range(total.bit_length() - 1):
        route = [(i, i ^ (1 << bit)) for i in range(total)]
        branch = jnp.where(apart == (1 << bit), bit + 1, branch)
        branches.append(lambda route=route: finished(route))
    return lax.switch(branch, branches)


def solution(mesh):
    in_specs = (
        P(None, ("group", "dev"), None),
        P(("group", "dev"), None),
        P(("group", "dev"), None),
        P(("group", "dev"), None),
        P(("group", "dev"), None),
        P(),
        P(("group", "dev")),
        P(("group", "dev")),
        P(("group", "dev")),
        P(("group", "dev")),
    )
    out_specs = (P(None, ("group", "dev"), None), P(("group", "dev"), None))
    return jax.shard_map(local, mesh=mesh, in_specs=in_specs, out_specs=out_specs, check_vma=False)
```

profile of v0, /device:TPU:6, one launch (start us, length us, event | category | flops | bytes accessed | tf_op | source)
XLA Modules:
  0.0 92.1 jit_solution(14709745011181140803)
XLA Ops:
  0.6 6.7 %pack.1 = (f32[4,256,128]{2,1,0:T(8,128)}, f32[8,128]{1,0:T(8,128)S(1)}, f32[496,128]{1,0:T(8,128)}, f32[496,128]{1,0:T(8,128)}, f32[296,128]{1,0:T(8,128)}, /*i...) custom-call(f32[6,512,128]{2,1,0:T(8,128)} %bitcast.98, ...), custom_call_target="tpu_custom_call" | custom-call | tf_op jit(solution)/shard_map/pack/pallas_call | solution.py:733
  7.3 0.6 collective-permute-start.10
  7.9 2.4 %collective-permute-start.11 = (f32[360,128]{1,0:T(8,128)}, f32[360,128]{1,0:T(8,128)S(1)}, u32[]{:S(2)}, u32[]{:S(2)}) collective-permute-start(f32[360,128]{1,0:T(8,128)} %get-tuple-element.366), channel_id=1, source_target_pairs={{0,8},{8,16},{16,24},{24,0},{1,9},{9,17},{17,25},{25,1},{2,10},{10... | collective-permute-start | bytes 552968 | tf_op jit(solution)/shard_map/ppermute | solution.py:698
  10.3 3.5 %collective-permute-start.13 = (f32[496,128]{1,0:T(8,128)}, f32[496,128]{1,0:T(8,128)S(1)}, u32[]{:S(2)}, u32[]{:S(2)}) collective-permute-start(f32[496,128]{1,0:T(8,128)} %get-tuple-element.376), channel_id=1, source_target_pairs={{0,7},{1,0},{2,1},{3,2},{4,3},{5,4},{6,5},{7,6},{8,15},{9,8},{10,9... | collective-permute-start | bytes 761864 | tf_op jit(solution)/shard_map/ppermute | solution.py:698
  13.8 1.8 %collective-permute-start.14 = (f32[296,128]{1,0:T(8,128)}, f32[296,128]{1,0:T(8,128)S(1)}, u32[]{:S(2)}, u32[]{:S(2)}) collective-permute-start(f32[296,128]{1,0:T(8,128)} %get-tuple-element.379), channel_id=1, source_target_pairs={{0,6},{1,7},{2,0},{3,1},{4,2},{5,3},{6,4},{7,5},{8,14},{9,15},{10,... | collective-permute-start | bytes 454664 | tf_op jit(solution)/shard_map/ppermute | solution.py:698
  15.7 4.7 %ions.1 = (f32[3,4,256,128]{3,2,1,0:T(8,128)S(1)}, f32[4,256,128]{2,1,0:T(8,128)S(1)}, f32[128,128]{1,0:T(8,128)}, f32[128,128]{1,0:T(8,128)}) custom-call(f32[6,512,128]{2,1,0:T(8,128)} %bitcast.99, s32[512,128]{1,0:T(8,128)} %bitcast.101, f32[512,128]{1,0:T(8,128)} %bitcast.103), custom_call_target="tpu_custom_call" | custom-call | tf_op jit(solution)/shard_map/ions/pallas_call | solution.py:754
  20.4 0.6 copy-done.17
  21.1 0.2 collective-permute-start.15
  21.3 2.2 %collective-permute-done.14.refs_2_.refs_12_ = f32[296,128]{1,0:T(8,128)S(1)} collective-permute-done((f32[296,128]{1,0:T(8,128)}, f32[296,128]{1,0:T(8,128)S(1)}, u32[]{:S(2)}, u32[]{:S(2)}) %collective-permute-start.14) | collective-permute-done | bytes 151584 | tf_op jit(solution)/shard_map/ppermute | solution.py:698
  23.5 4.7 %collective-permute-done.16.refs_4_.refs_14_ = f32[72,128]{1,0:T(8,128)S(1)} collective-permute-done((f32[72,128]{1,0:T(8,128)S(1)}, f32[72,128]{1,0:T(8,128)S(1)}, u32[]{:S(2)}, u32[]{:S(2)}) %collective-permute-start.16) | collective-permute-done | bytes 36896 | tf_op jit(solution)/shard_map/ppermute | solution.py:698
  28.2 0.6 collective-permute-done.17.refs_5_.refs_15_
  28.9 0.3 relay.1
  29.3 0.1 collective-permute-start.22
  29.4 0.3 copy-done.11
  29.6 2.6 %collective-permute-start.23 = (f32[288,128]{1,0:T(8,128)S(1)}, f32[288,128]{1,0:T(8,128)S(1)}, u32[]{:S(2)}, u32[]{:S(2)}) collective-permute-start(f32[288,128]{1,0:T(8,128)S(1)} %get-tuple-element.393), channel_id=1, source_target_pairs={{0,8},{8,16},{16,24},{24,0},{1,9},{9,17},{17,25},{25,1},{2,10},{10... | collective-permute-start | bytes 442376 | tf_op jit(solution)/shard_map/ppermute | solution.py:698
  32.3 1.3 %ion_z_faces.1 = (f32[128,128]{1,0:T(8,128)S(1)}, f32[128,128]{1,0:T(8,128)S(1)}) custom-call(f32[3,4,256,128]{3,2,1,0:T(8,128)S(1)} %get-tuple-element.372.sp, f32[4,256,128]{2,1,0:T(8,128)S(1)} %get-tuple-element.373.wd), custom_call_target="tpu_custom_call" | custom-call | tf_op jit(solution)/shard_map/ion_z_faces/pallas_call | solution.py:767
  33.6 0.1 collective-permute-start.20
  33.6 2.9 %collective-permute-start.21 = (f32[128,128]{1,0:T(8,128)S(1)}, f32[128,128]{1,0:T(8,128)S(1)}, u32[]{:S(2)}, u32[]{:S(2)}) collective-permute-start(f32[128,128]{1,0:T(8,128)S(1)} %get-tuple-element.388), channel_id=1, source_target_pairs={{0,8},{8,16},{16,24},{24,0},{1,9},{9,17},{17,25},{25,1},{2,10},{10... | collective-permute-start | bytes 196616 | tf_op jit(solution)/shard_map/ppermute | solution.py:698
  36.6 1.7 %collective-permute-start.18 = (f32[128,128]{1,0:T(8,128)S(1)}, f32[128,128]{1,0:T(8,128)S(1)}, u32[]{:S(2)}, u32[]{:S(2)}) collective-permute-start(f32[128,128]{1,0:T(8,128)S(1)} %copy-done.26), channel_id=1, source_target_pairs={{0,2},{1,3},{2,4},{3,5},{4,6},{5,7},{6,0},{7,1},{8,10},{9,11},{10,... | collective-permute-start | bytes 196616 | tf_op jit(solution)/shard_map/ppermute | solution.py:698
  38.3 2.9 %collective-permute-done.20.refs_8_ = f32[128,128]{1,0:T(8,128)S(1)} collective-permute-done((f32[128,128]{1,0:T(8,128)S(1)}, f32[128,128]{1,0:T(8,128)S(1)}, u32[]{:S(2)}, u32[]{:S(2)}) %collective-permute-start.20) | collective-permute-done | bytes 65568 | tf_op jit(solution)/shard_map/ppermute | solution.py:698
  41.2 1.6 %collective-permute-start.19 = (f32[128,128]{1,0:T(8,128)S(1)}, f32[128,128]{1,0:T(8,128)S(1)}, u32[]{:S(2)}, u32[]{:S(2)}) collective-permute-start(f32[128,128]{1,0:T(8,128)S(1)} %copy-done.25), channel_id=1, source_target_pairs={{0,6},{1,7},{2,0},{3,1},{4,2},{5,3},{6,4},{7,5},{8,14},{9,15},{10,... | collective-permute-start | bytes 196616 | tf_op jit(solution)/shard_map/ppermute | solution.py:698
  44.1 1.6 %collective-permute-done.19.refs_7_ = f32[128,128]{1,0:T(8,128)S(1)} collective-permute-done((f32[128,128]{1,0:T(8,128)S(1)}, f32[128,128]{1,0:T(8,128)S(1)}, u32[]{:S(2)}, u32[]{:S(2)}) %collective-permute-start.19) | collective-permute-done | bytes 65568 | tf_op jit(solution)/shard_map/ppermute | solution.py:698
  45.8 0.6 copy-done.15
  46.4 0.1 copy-done.19
  46.5 21.2 %sweeps.1 = (f32[4,256,128]{2,1,0:T(8,128)S(1)}, f32[4,544,128]{2,1,0:T(8,128)S(1)}, f32[7,128,128]{2,1,0:T(8,128)}, f32[7,128,128]{2,1,0:T(8,128)}) custom-call(f32[8,128]{1,0:T(8,128)S(1)} %get-tuple-element.374.refs_0_, f32[4,256,128]{2,1,0:T(8,128)} %get-tuple-element.389.refs_1_, f32[360,128]{1,0:T(8,128)} %copy-done.17, f32[360,128]{1,0:T(8,128)} %copy-done.18, ...), custom_call_target="tpu_custom_call" | custom-call | tf_op jit(solution)/shard_map/sweeps/pallas_call | solution.py:803
  67.8 24.3 %conditional.1 = (f32[6,2,32768]{2,1,0:T(2,128)}, f32[2,32768]{1,0:T(2,128)}) conditional(s32[]{:T(128)} %clamp.3, (f32[3,4,32,8,128]{4,3,2,1,0:T(8,128)S(1)}, f32[4,32,8,128]{3,2,1,0:T(8,128)S(1)}, f32[8,128]{1,0:T(8,128)S(1)}, f32[496,128]{1,0:T(8,128)}, f32[496,128]{1,0:T(8,128)}, /*index=5*/f32[128,128]{1,0:T(8,128)}, ...), branch_computations={%region_0.1_spmd, %region_1.2_spmd, %region_2.3_spmd, %region_3.4_... | conditional | bytes 5505148 | solution.py:876
  67.8 0.1 collective-permute-start.6
  67.9 6.8 %update.10 = (f32[7,128,128]{2,1,0:T(8,128)S(1)}, f32[7,128,128]{2,1,0:T(8,128)S(1)}) custom-call(f32[3,4,32,8,128]{4,3,2,1,0:T(8,128)S(1)} %get-tuple-element.290.sp, f32[4,32,8,128]{3,2,1,0:T(8,128)S(1)} %get-tuple-element.291.wd, f32[8,128]{1,0:T(8,128)S(1)} %get-tuple-element.292.refs_0_, f32[496,128]{1,0:T(8,128)} %get-tuple-element.293.refs_1_, ...), custom_call_target="tpu_custom_call" | custom-call | tf_op jit(solution)/shard_map/cond/branch_4_fun/update/pallas_call | solution.py:836
  74.7 2.1 %collective-permute-start.7 = (f32[7,128,128]{2,1,0:T(8,128)S(1)}, f32[7,128,128]{2,1,0:T(8,128)S(1)}, u32[]{:S(2)}, u32[]{:S(2)}) collective-permute-start(f32[7,128,128]{2,1,0:T(8,128)S(1)} %get-tuple-element.306), channel_id=1, source_target_pairs={{0,8},{1,9},{2,10},{3,11},{4,12},{5,13},{6,14},{7,15},{8,0},{9,1},... | collective-permute-start | bytes 1376264 | tf_op jit(solution)/shard_map/cond/branch_4_fun/ppermute | solution.py:862
  76.8 4.7 %collective-permute-done.6.refs_2_ = f32[7,128,128]{2,1,0:T(8,128)S(1)} collective-permute-done((f32[7,128,128]{2,1,0:T(8,128)}, f32[7,128,128]{2,1,0:T(8,128)S(1)}, u32[]{:S(2)}, u32[]{:S(2)}) %collective-permute-start.6) | collective-permute-done | bytes 458784 | tf_op jit(solution)/shard_map/cond/branch_4_fun/ppermute | solution.py:862
  81.5 8.6 %collective-permute-done.7.refs_3_ = f32[7,128,128]{2,1,0:T(8,128)S(1)} collective-permute-done((f32[7,128,128]{2,1,0:T(8,128)S(1)}, f32[7,128,128]{2,1,0:T(8,128)S(1)}, u32[]{:S(2)}, u32[]{:S(2)}) %collective-permute-start.7) | collective-permute-done | bytes 458784 | tf_op jit(solution)/shard_map/cond/branch_4_fun/ppermute | solution.py:862
  90.1 2.0 %place.10 = (f32[6,512,128]{2,1,0:T(8,128)}, f32[512,128]{1,0:T(8,128)}) custom-call(s32[1]{0:T(128)} %get-tuple-element.288.refs_12_.give_slot, f32[7,128,128]{2,1,0:T(8,128)S(1)} %copy-done.8, f32[7,128,128]{2,1,0:T(8,128)S(1)} %get-tuple-element.304.refs_1_, f32[7,128,128]{2,1,0:T(8,128)S(1)} %collective-permute-done.6.refs_2_, ...), custom_call_target="tpu_custom_call" | custom-call | tf_op jit(solution)/shard_map/cond/branch_4_fun/place/pallas_call | solution.py:851
  (54 shorter events, 0.2 us)
Async XLA Ops:
  7.3 13.8 %copy-start.24 = (f32[296,128]{1,0:T(8,128)S(1)}, f32[296,128]{1,0:T(8,128)}, u32[]{:S(2)}) copy-start(f32[296,128]{1,0:T(8,128)} %get-tuple-element.380) | copy-start | bytes 454660
  7.3 14.0 %copy-start.28 = (f32[72,128]{1,0:T(8,128)S(1)}, f32[72,128]{1,0:T(8,128)}, u32[]{:S(2)}) copy-start(f32[72,128]{1,0:T(8,128)} %get-tuple-element.381) | copy-start | bytes 110596
  7.3 16.2 %copy-start.27 = (f32[72,128]{1,0:T(8,128)S(1)}, f32[72,128]{1,0:T(8,128)}, u32[]{:S(2)}) copy-start(f32[72,128]{1,0:T(8,128)} %get-tuple-element.382) | copy-start | bytes 110596
  7.3 13.1 %collective-permute-start.10 = (f32[360,128]{1,0:T(8,128)}, f32[360,128]{1,0:T(8,128)S(1)}, u32[]{:S(2)}, u32[]{:S(2)}) collective-permute-start(f32[360,128]{1,0:T(8,128)} %get-tuple-element.365), channel_id=1, source_target_pairs={{0,24},{8,0},{16,8},{24,16},{1,25},{9,1},{17,9},{25,17},{2,26},{10... | collective-permute-start | bytes 552968 | tf_op jit(solution)/shard_map/ppermute | solution.py:698
  7.9 12.5 %collective-permute-start.11 = (f32[360,128]{1,0:T(8,128)}, f32[360,128]{1,0:T(8,128)S(1)}, u32[]{:S(2)}, u32[]{:S(2)}) collective-permute-start(f32[360,128]{1,0:T(8,128)} %get-tuple-element.366), channel_id=1, source_target_pairs={{0,8},{8,16},{16,24},{24,0},{1,9},{9,17},{17,25},{25,1},{2,10},{10... | collective-permute-start | bytes 552968 | tf_op jit(solution)/shard_map/ppermute | solution.py:698
  10.3 18.6 %collective-permute-start.12 = (f32[496,128]{1,0:T(8,128)}, f32[496,128]{1,0:T(8,128)S(1)}, u32[]{:S(2)}, u32[]{:S(2)}) collective-permute-start(f32[496,128]{1,0:T(8,128)} %get-tuple-element.375), channel_id=1, source_target_pairs={{0,1},{1,2},{2,3},{3,4},{4,5},{5,6},{6,7},{7,0},{8,9},{9,10},{10,1... | collective-permute-start | bytes 761864 | tf_op jit(solution)/shard_map/ppermute | solution.py:698
  10.3 18.6 %collective-permute-start.13 = (f32[496,128]{1,0:T(8,128)}, f32[496,128]{1,0:T(8,128)S(1)}, u32[]{:S(2)}, u32[]{:S(2)}) collective-permute-start(f32[496,128]{1,0:T(8,128)} %get-tuple-element.376), channel_id=1, source_target_pairs={{0,7},{1,0},{2,1},{3,2},{4,3},{5,4},{6,5},{7,6},{8,15},{9,8},{10,9... | collective-permute-start | bytes 761864 | tf_op jit(solution)/shard_map/ppermute | solution.py:698
  13.8 9.7 %collective-permute-start.14 = (f32[296,128]{1,0:T(8,128)}, f32[296,128]{1,0:T(8,128)S(1)}, u32[]{:S(2)}, u32[]{:S(2)}) collective-permute-start(f32[296,128]{1,0:T(8,128)} %get-tuple-element.379), channel_id=1, source_target_pairs={{0,6},{1,7},{2,0},{3,1},{4,2},{5,3},{6,4},{7,5},{8,14},{9,15},{10,... | collective-permute-start | bytes 454664 | tf_op jit(solution)/shard_map/ppermute | solution.py:698
  20.3 16.2 %copy-start.26 = (f32[128,128]{1,0:T(8,128)S(1)}, f32[128,128]{1,0:T(8,128)}, u32[]{:S(2)}) copy-start(f32[128,128]{1,0:T(8,128)} %get-tuple-element.385) | copy-start | bytes 196612
  20.4 20.8 %copy-start.25 = (f32[128,128]{1,0:T(8,128)S(1)}, f32[128,128]{1,0:T(8,128)}, u32[]{:S(2)}) copy-start(f32[128,128]{1,0:T(8,128)} %get-tuple-element.386) | copy-start | bytes 196612
  20.4 26.1 %copy-start.21 = (f32[6]{0:T(128)S(1)}, f32[6]{0:T(128)}, u32[]{:S(2)}) copy-start(f32[6]{0:T(128)} %refs_18_.1) | copy-start | bytes 76
  20.4 26.1 %copy-start.22 = (f32[2]{0:T(128)S(1)}, f32[2]{0:T(128)}, u32[]{:S(2)}) copy-start(f32[2]{0:T(128)} %refs_19_.1) | copy-start | bytes 28
  20.4 26.1 %copy-start.23 = (s32[2]{0:T(128)S(1)}, s32[2]{0:T(128)}, u32[]{:S(2)}) copy-start(s32[2]{0:T(128)} %refs_20_.1) | copy-start | bytes 28
  20.4 8.5 %copy-start.18 = (f32[360,128]{1,0:T(8,128)}, f32[360,128]{1,0:T(8,128)S(1)}, u32[]{:S(2)}) copy-start(f32[360,128]{1,0:T(8,128)S(1)} %collective-permute-done.11.refs_3_) | copy-start | bytes 552964
  21.1 7.8 %collective-permute-start.15 = (f32[296,128]{1,0:T(8,128)S(1)}, f32[296,128]{1,0:T(8,128)S(1)}, u32[]{:S(2)}, u32[]{:S(2)}) collective-permute-start(f32[296,128]{1,0:T(8,128)S(1)} %copy-done.24), channel_id=1, source_target_pairs={{0,2},{1,3},{2,4},{3,5},{4,6},{5,7},{6,0},{7,1},{8,10},{9,11},{10,... | collective-permute-start | bytes 454664 | tf_op jit(solution)/shard_map/ppermute | solution.py:698
  21.3 6.9 %collective-permute-start.16 = (f32[72,128]{1,0:T(8,128)S(1)}, f32[72,128]{1,0:T(8,128)S(1)}, u32[]{:S(2)}, u32[]{:S(2)}) collective-permute-start(f32[72,128]{1,0:T(8,128)S(1)} %copy-done.28), channel_id=1, source_target_pairs={{0,5},{1,6},{2,7},{3,0},{4,1},{5,2},{6,3},{7,4},{8,13},{9,14},{10,... | collective-permute-start | bytes 110600 | tf_op jit(solution)/shard_map/ppermute | solution.py:698
  23.5 22.9 %copy-start = (f32[296,128]{1,0:T(8,128)}, f32[296,128]{1,0:T(8,128)S(1)}, u32[]{:S(2)}) copy-start(f32[296,128]{1,0:T(8,128)S(1)} %collective-permute-done.14.refs_2_.refs_12_) | copy-start | bytes 454660
  23.5 5.3 %collective-permute-start.17 = (f32[72,128]{1,0:T(8,128)S(1)}, f32[72,128]{1,0:T(8,128)S(1)}, u32[]{:S(2)}, u32[]{:S(2)}) collective-permute-start(f32[72,128]{1,0:T(8,128)S(1)} %copy-done.27), channel_id=1, source_target_pairs={{0,3},{1,4},{2,5},{3,6},{4,7},{5,0},{6,1},{7,2},{8,11},{9,12},{10,... | collective-permute-start | bytes 110600 | tf_op jit(solution)/shard_map/ppermute | solution.py:698
  28.2 18.3 %copy-start.2 = (f32[72,128]{1,0:T(8,128)}, f32[72,128]{1,0:T(8,128)S(1)}, u32[]{:S(2)}) copy-start(f32[72,128]{1,0:T(8,128)S(1)} %collective-permute-done.16.refs_4_.refs_14_) | copy-start | bytes 110596
  28.9 17.6 %copy-start.3 = (f32[72,128]{1,0:T(8,128)}, f32[72,128]{1,0:T(8,128)S(1)}, u32[]{:S(2)}) copy-start(f32[72,128]{1,0:T(8,128)S(1)} %collective-permute-done.17.refs_5_.refs_15_) | copy-start | bytes 110596
  28.9 12.3 %copy-start.10 = (f32[496,128]{1,0:T(8,128)}, f32[496,128]{1,0:T(8,128)S(1)}, u32[]{:S(2)}) copy-start(f32[496,128]{1,0:T(8,128)S(1)} %collective-permute-done.12.refs_1_.refs_11_) | copy-start | bytes 761860
  28.9 17.6 %copy-start.1 = (f32[296,128]{1,0:T(8,128)}, f32[296,128]{1,0:T(8,128)S(1)}, u32[]{:S(2)}) copy-start(f32[296,128]{1,0:T(8,128)S(1)} %collective-permute-done.15.refs_3_.refs_13_) | copy-start | bytes 454660
  29.3 16.5 %collective-permute-start.22 = (f32[288,128]{1,0:T(8,128)S(1)}, f32[288,128]{1,0:T(8,128)S(1)}, u32[]{:S(2)}, u32[]{:S(2)}) collective-permute-start(f32[288,128]{1,0:T(8,128)S(1)} %get-tuple-element.392), channel_id=1, source_target_pairs={{0,24},{8,0},{16,8},{24,16},{1,25},{9,1},{17,9},{25,17},{2,26},{10... | collective-permute-start | bytes 442376 | tf_op jit(solution)/shard_map/ppermute | solution.py:698
  29.6 16.1 %collective-permute-start.23 = (f32[288,128]{1,0:T(8,128)S(1)}, f32[288,128]{1,0:T(8,128)S(1)}, u32[]{:S(2)}, u32[]{:S(2)}) collective-permute-start(f32[288,128]{1,0:T(8,128)S(1)} %get-tuple-element.393), channel_id=1, source_target_pairs={{0,8},{8,16},{16,24},{24,0},{1,9},{9,17},{17,25},{25,1},{2,10},{10... | collective-permute-start | bytes 442376 | tf_op jit(solution)/shard_map/ppermute | solution.py:698
  33.6 7.6 %collective-permute-start.20 = (f32[128,128]{1,0:T(8,128)S(1)}, f32[128,128]{1,0:T(8,128)S(1)}, u32[]{:S(2)}, u32[]{:S(2)}) collective-permute-start(f32[128,128]{1,0:T(8,128)S(1)} %get-tuple-element.387), channel_id=1, source_target_pairs={{0,24},{8,0},{16,8},{24,16},{1,25},{9,1},{17,9},{25,17},{2,26},{10... | collective-permute-start | bytes 196616 | tf_op jit(solution)/shard_map/ppermute | solution.py:698
  33.6 10.5 %collective-permute-start.21 = (f32[128,128]{1,0:T(8,128)S(1)}, f32[128,128]{1,0:T(8,128)S(1)}, u32[]{:S(2)}, u32[]{:S(2)}) collective-permute-start(f32[128,128]{1,0:T(8,128)S(1)} %get-tuple-element.388), channel_id=1, source_target_pairs={{0,8},{8,16},{16,24},{24,0},{1,9},{9,17},{17,25},{25,1},{2,10},{10... | collective-permute-start | bytes 196616 | tf_op jit(solution)/shard_map/ppermute | solution.py:698
  36.6 7.6 %collective-permute-start.18 = (f32[128,128]{1,0:T(8,128)S(1)}, f32[128,128]{1,0:T(8,128)S(1)}, u32[]{:S(2)}, u32[]{:S(2)}) collective-permute-start(f32[128,128]{1,0:T(8,128)S(1)} %copy-done.26), channel_id=1, source_target_pairs={{0,2},{1,3},{2,4},{3,5},{4,6},{5,7},{6,0},{7,1},{8,10},{9,11},{10,... | collective-permute-start | bytes 196616 | tf_op jit(solution)/shard_map/ppermute | solution.py:698
  41.2 4.6 %collective-permute-start.19 = (f32[128,128]{1,0:T(8,128)S(1)}, f32[128,128]{1,0:T(8,128)S(1)}, u32[]{:S(2)}, u32[]{:S(2)}) collective-permute-start(f32[128,128]{1,0:T(8,128)S(1)} %copy-done.25), channel_id=1, source_target_pairs={{0,6},{1,7},{2,0},{3,1},{4,2},{5,3},{6,4},{7,5},{8,14},{9,15},{10,... | collective-permute-start | bytes 196616 | tf_op jit(solution)/shard_map/ppermute | solution.py:698
  44.1 1.6 %copy-start.13 = (f32[128,128]{1,0:T(8,128)}, f32[128,128]{1,0:T(8,128)S(1)}, u32[]{:S(2)}) copy-start(f32[128,128]{1,0:T(8,128)S(1)} %collective-permute-done.21.refs_9_) | copy-start | bytes 196612
  67.8 13.7 %collective-permute-start.6 = (f32[7,128,128]{2,1,0:T(8,128)}, f32[7,128,128]{2,1,0:T(8,128)S(1)}, u32[]{:S(2)}, u32[]{:S(2)}) collective-permute-start(f32[7,128,128]{2,1,0:T(8,128)} %get-tuple-element.305), channel_id=1, source_target_pairs={{0,8},{1,9},{2,10},{3,11},{4,12},{5,13},{6,14},{7,15},{8,0},{9,1},... | collective-permute-start | bytes 1376264 | tf_op jit(solution)/shard_map/cond/branch_4_fun/ppermute | solution.py:862
  67.9 22.2 %copy-start.8 = (f32[7,128,128]{2,1,0:T(8,128)S(1)}, f32[7,128,128]{2,1,0:T(8,128)}, u32[]{:S(2)}) copy-start(f32[7,128,128]{2,1,0:T(8,128)} %get-tuple-element.289.refs_0_) | copy-start | bytes 1376260 | tf_op jit(solution)/shard_map/cond
  74.7 15.4 %collective-permute-start.7 = (f32[7,128,128]{2,1,0:T(8,128)S(1)}, f32[7,128,128]{2,1,0:T(8,128)S(1)}, u32[]{:S(2)}, u32[]{:S(2)}) collective-permute-start(f32[7,128,128]{2,1,0:T(8,128)S(1)} %get-tuple-element.306), channel_id=1, source_target_pairs={{0,8},{1,9},{2,10},{3,11},{4,12},{5,13},{6,14},{7,15},{8,0},{9,1},... | collective-permute-start | bytes 1376264 | tf_op jit(solution)/shard_map/cond/branch_4_fun/ppermute | solution.py:862
  (7 other events, 6.7 us)
where the time goes:
time: 92.4 us; the launch traced here: 92.1 us
  Pallas kernels  43 us (47%)
  waiting for transfers between devices  25.3 us (27%)
  starting transfers between devices  19.7 us (21%)
  between operations  2.24 us (2%)
  local copies, waits for them, and re-layouts  1.72 us (2%)
    pallas_call x1, Pallas kernels, local(): pl.pallas_call(functools.partial(sweep_kernel, pieces), out_shape=(f32(QU...  21.2 us
    ppermute x14, starting transfers between devices, moved(): return lax.ppermute(block, axis, [(i, (i + offset) % n) for i in range(n)])  17.5 us
    ppermute x2, waiting for transfers between devices, finished(): lax.ppermute(block, ('group', 'dev'), route)  13.3 us
    ppermute x14, waiting for transfers between devices, moved(): return lax.ppermute(block, axis, [(i, (i + offset) % n) for i in range(n)])  12 us
    pallas_call x1, Pallas kernels, second_half(): pl.pallas_call(functools.partial(update_kernel, 1, x_starts), out_shape=h...  6.82 us
    pallas_call x1, Pallas kernels, local(): pl.pallas_call(functools.partial(pack_kernel, pieces), out_shape=(f32(QUA...  6.66 us
    pallas_call x1, Pallas kernels, local(): pl.pallas_call(ions_kernel, out_shape=(f32(PAIRS, QUADS, PLANE, LANES), f...  4.68 us
    ppermute x2, starting transfers between devices, finished(): lax.ppermute(block, ('group', 'dev'), route)  2.14 us
  transfers between devices with their start and end apart: 16, of which 7 were waited for; matrix products, arithmetic and copies ran while one was open for 0% of the time, Pallas kernels for 14%

commit v1 on v0

--- a/solution.py
+++ b/solution.py
@@ -26,7 +26,7 @@
 HALF = SIDE // 2
 
 FACE_TBL = DEPTH * SIDE
-Y_ROWS = FACE_TBL + 8
+Y_ION = FACE_TBL + 8
 EDGE_TBL = 64
 EDGE_ROWS = EDGE_TBL + 8
 THIRD = 11
@@ -34,11 +34,12 @@
 ZC_ROWS = ZC_TBL + 8
 ZH_EDGE = 2 * 3 * SIDE
 ZH_TBL = ZH_EDGE + 64
-ZH_ROWS = ZH_TBL + 32
+ZH_ION = ZH_TBL + 32
 FIELDS = PAIRS + 1
 ION_ROWS = FIELDS * SIDE
-X_ROWS = Y_ROWS + ION_ROWS
+Y_ROWS = Y_ION + ION_ROWS
 BLOCKS = SIDE // FIELDS
+ZH_ROWS = ZH_ION + ION_ROWS
 
 ZH_PLACE = {
     (n, l): (n, off) if l < 5 else (2, 6 * n + off)
@@ -171,6 +172,20 @@
             for j in range(QUADS):
                 ref[start + k * SIDE + j * 8 : start + k * SIDE + j * 8 + 8, :] = planes[j]
 
+    group = lane_of(SIDE) >> 5
+
+    def ion_rows(y, ref, start):
+        for k in range(FIELDS):
+            v = jnp.zeros((SIDE, LANES), jnp.float32)
+            for b in range(2):
+                rows = pl.ds(y // 4 * 2 + b, SIDE, stride=16)
+                if k == PAIRS:
+                    wet = pore[rows, :].astype(jnp.float32) * openness[rows, :]
+                for f in range(2):
+                    native = species[k + f * PAIRS, rows, :] if k < PAIRS else wet
+                    v = jnp.where(group == 2 * b + f, roll(native, (2 * b + f - y % 4) * SIDE), v)
+            ref[start + k * SIDE : start + (k + 1) * SIDE, :] = v
+
     for sx, sy in SIDES:
         ref, base = where[(sx, sy)]
         for l in range(DEPTH):
@@ -181,9 +196,11 @@
             else:
                 y = l if sy < 0 else SIDE - 1 - l
                 ref[base + l * SIDE : base + (l + 1) * SIDE, :] = pd[y % 4, pl.ds(y // 4, SIDE, stride=8), :]
-        ref[base + FACE_TBL : base + Y_ROWS, :] = table
+        ref[base + FACE_TBL : base + Y_ION, :] = table
         if sx:
-            ion_planes(0 if sx < 0 else SIDE - 1, ref, base + Y_ROWS)
+            ion_planes(0 if sx < 0 else SIDE - 1, ref, base + Y_ION)
+        else:
+            ion_rows(0 if sy < 0 else SIDE - 1, ref, base + Y_ION)
     for sx, sy in CORNERS:
         ref, base = where[(sx, sy)]
         x0 = 0 if sx < 0 else SIDE - 8
@@ -201,7 +218,7 @@
     return fields + [swap_groups((w[0], w[0], w[1], w[1]), lane)]
 
 
-def ions_kernel(species_in, pore_in, openness_in, sp, wd, ylo, yhi, species, pore, openness, sems):
+def ions_kernel(species_in, pore_in, openness_in, sp, wd, species, pore, openness, sems):
     parts = []
     for part in range(2):
         rows = pl.ds(part * PLANE, PLANE)
@@ -229,10 +246,6 @@
         for c in parts[part]:
             c.wait()
         lax.fori_loop(part * HALF, (part + 1) * HALF, step, 0, unroll=2)
-    for k in range(FIELDS):
-        for y, ref in ((0, ylo), (SIDE - 1, yhi)):
-            at = pl.ds(y // 4, SIDE, stride=8)
-            ref[k * SIDE : (k + 1) * SIDE, :] = sp[k, y % 4, at, :] if k < PAIRS else wd[y % 4, at, :]
 
 
 def ion_z_kernel(sp, wd, zlo, zhi):
@@ -256,7 +269,9 @@
 
 
 def relay_kernel(pieces, *refs):
-    arrived, (zl, zh) = refs[:-2], refs[-2:]
+    arrived, (ions_lo, ions_hi, zl, zh) = refs[:-5], refs[-4:]
+    zl[ZH_ION:, :] = ions_lo[...]
+    zh[ZH_ION:, :] = ions_hi[...]
     where = {name: (arrived[k], base) for k, held in enumerate(pieces) for name, base in held}
     lane32 = lane_of(SIDE) & 31
     for axis in range(2):
@@ -272,8 +287,8 @@
                 lo[block] = jnp.where((lane32 >= off) & (lane32 < off + width), roll(v, off), lo[block])
                 hi[block] = jnp.where((lane32 <= 31 - off) & (lane32 > 31 - off - width), roll(v, -off), hi[block])
             at = slice(ZH_TBL + (2 * axis + n) * 8, ZH_TBL + (2 * axis + n) * 8 + 8)
-            zl[at, :] = ref[base + FACE_TBL : base + Y_ROWS, :]
-            zh[at, :] = ref[base + FACE_TBL : base + Y_ROWS, :]
+            zl[at, :] = ref[base + FACE_TBL : base + Y_ION, :]
+            zh[at, :] = ref[base + FACE_TBL : base + Y_ION, :]
         for block in range(3):
             at = slice((axis * 3 + block) * SIDE, (axis * 3 + block + 1) * SIDE)
             zl[at, :] = lo[block]
@@ -291,7 +306,7 @@
 
 
 def sweep_kernel(pieces, *refs):
-    n_in = 10 + len(pieces)
+    n_in = 6 + len(pieces)
     sources, (sp, wd), scalars = refs[:n_in], refs[n_in : n_in + 2], refs[n_in + 2 : n_in + 6]
     ud, fd, keep, send = refs[n_in + 6 : n_in + 10]
     ua, ub, dn, mx, myp, mym, se_cube, we_cube, zw, udv, fdv, sems, ion_sems, out_sems = refs[n_in + 10 : n_in + 24]
@@ -303,7 +318,7 @@
     for c in late:
         c.start()
     own, pd, zup, zdn, zhup, zhdn = held[:6]
-    yz_halos, arrived = held[6:10], held[10:]
+    arrived = held[6:]
     where = {name: (arrived[k], base) for k, held in enumerate(pieces) for name, base in held}
 
     lane = lane_of(8)
@@ -318,7 +333,7 @@
     ztable = {1: {(0, 0): zup[ZC_TBL:, :]}, -1: {(0, 0): zdn[ZC_TBL:, :]}}
     for number, (sx, sy) in enumerate(SIDES):
         ref, base = where[(-sx, -sy)]
-        table[(sx, sy)] = ref[base + FACE_TBL : base + Y_ROWS, :]
+        table[(sx, sy)] = ref[base + FACE_TBL : base + Y_ION, :]
         for sz, held in ((1, zhup), (-1, zhdn)):
             ztable[sz][(sx, sy)] = held[ZH_TBL + number * 8 : ZH_TBL + number * 8 + 8, :]
     for sx, sy in CORNERS:
@@ -496,8 +511,8 @@
         c.start()
     for c in late:
         c.wait()
-    x_halos = [(ref, start + Y_ROWS) for ref, start in (where[(1, 0)], where[(-1, 0)])]
-    update_half(0, se_cube, we_cube, zw, own, *x_halos, *yz_halos, udv, fdv, *scalars, keep, send)
+    halos = [(ref, start + Y_ION) for ref, start in (where[(1, 0)], where[(-1, 0)], where[(0, 1)], where[(0, -1)])]
+    update_half(0, se_cube, we_cube, zw, own, *halos, zhup, zhdn, udv, fdv, *scalars, keep, send)
     for c in back:
         c.wait()
 
@@ -510,7 +525,7 @@
     return copies
 
 
-def update_kernel(half, x_starts, sp, wd, *refs):
+def update_kernel(half, starts, sp, wd, *refs):
     sources, scalars, outs = refs[:9], refs[9:13], refs[13:15]
     se_cube, we_cube, zw, sems = refs[15:19]
     held = refs[19:]
@@ -520,8 +535,9 @@
         c.start()
     for c in copies:
         c.wait()
-    own, xdn, xup, *others = held
-    update_half(half, se_cube, we_cube, zw, own, (xdn, x_starts[0]), (xup, x_starts[1]), *others, *scalars, *outs)
+    own, *others = held
+    halos = list(zip(others[:4], starts))
+    update_half(half, se_cube, we_cube, zw, own, *halos, *others[4:], *scalars, *outs)
 
 
 def update_half(
@@ -570,14 +586,14 @@
         v = turned(ref[start + k * SIDE : start + (k + 1) * SIDE, :], way)
         for j in range(QUADS):
             put(k, j, slice(layer * SPAN + 4, layer * SPAN + 12), v[j * 8 : j * 8 + 8])
-        rows = slice(k * SIDE + x0, k * SIDE + x0 + HALF)
-        put(k, 0, pl.ds(SPAN + 12, HALF, stride=SPAN), turned(yup[rows, :], 2))
-        put(k, 3, pl.ds(SPAN + 3, HALF, stride=SPAN), turned(ydn[rows, :], 3))
+        for j, row, way, (ref, start) in ((0, 12, 2, yup), (3, 3, 3, ydn)):
+            rows = slice(start + k * SIDE + x0, start + k * SIDE + x0 + HALF)
+            put(k, j, pl.ds(SPAN + row, HALF, stride=SPAN), turned(ref[rows, :], way))
 
     odd = (lane & 1) == 1
     for j in range(QUADS):
         for i in range(FIELDS):
-            rows = slice(j * SIDE + i * 8, j * SIDE + i * 8 + 8)
+            rows = slice(ZH_ION + j * SIDE + i * 8, ZH_ION + j * SIDE + i * 8 + 8)
             zu = turned(zup[rows, :], 4)
             zd = roll(turned(zdn[rows, :], 5), -31)
             both = (jnp.where(odd, zd, zu), jnp.where(odd, zu, zd))
@@ -719,7 +735,7 @@
         offset = (sx + sy * stride) % dev_count
         offset = offset if offset <= dev_count // 2 else offset - dev_count
         rows, pieces = held.get(offset, (0, ()))
-        held[offset] = (rows + (X_ROWS if sy == 0 else Y_ROWS if sx == 0 else EDGE_ROWS), pieces + (((sx, sy), rows),))
+        held[offset] = (rows + (Y_ROWS if 0 in (sx, sy) else EDGE_ROWS), pieces + (((sx, sy), rows),))
     offsets = sorted(held, key=lambda o: (-held[o][0], -abs(o), o))
     pieces = tuple(held[o][1] for o in offsets)
 
@@ -746,23 +762,24 @@
         name="pack",
     )(species_rows, rows_of(potential), pore_rows, openness_rows, neighbours)
     faces = [k for k, o in enumerate(offsets) if held[o][0] >= Y_ROWS]
-    rest = faces[-1:] + [k for k in range(len(offsets)) if k not in faces]
+    lone = [k for k in range(len(offsets)) if k not in faces]
+    rest = faces[-1:] + lone[1:]
     zup = moved(down, "group", -1)
-    zdn = moved(up, "group", 1)
-    arrived = {k: moved(blocks[k], "dev", offsets[k]) for k in faces[:-1]}
-
-    sp, wd, ydown, yup = pl.pallas_call(
+    arrived = {k: moved(blocks[k], "dev", offsets[k]) for k in faces[:-1] + lone[:1]}
+
+    sp, wd = pl.pallas_call(
         ions_kernel,
-        out_shape=(f32(PAIRS, QUADS, PLANE, LANES), f32(QUADS, PLANE, LANES), *([f32(ION_ROWS, LANES)] * 2)),
+        out_shape=(f32(PAIRS, QUADS, PLANE, LANES), f32(QUADS, PLANE, LANES)),
         in_specs=[HBM] * 3,
-        out_specs=(VMEM,) * 4,
+        out_specs=(VMEM,) * 2,
         scratch_shapes=[fields, field_int, field, pltpu.SemaphoreType.DMA((2, 3))],
         compiler_params=grant(60),
         name="ions",
     )(species_rows, pore_rows, openness_rows)
 
-    zup, zdn, sp, wd, *more = lax.optimization_barrier((zup, zdn, sp, wd, *(blocks[k] for k in rest)))
+    zup, up, sp, wd, *more = lax.optimization_barrier((zup, up, sp, wd, *(blocks[k] for k in rest)))
     arrived.update((k, moved(block, "dev", offsets[k])) for k, block in zip(rest, more))
+    zdn = moved(up, "group", 1)
 
     zdown, zupper = pl.pallas_call(
         ion_z_kernel,
@@ -773,22 +790,18 @@
         name="ion_z_faces",
     )(sp, wd)
 
-    z_halos = [moved(zdown, "group", -1), moved(zupper, "group", 1)]
     arrived = [arrived[k] for k in range(len(offsets))]
 
     zl, zh = pl.pallas_call(
         functools.partial(relay_kernel, pieces),
         out_shape=(f32(ZH_ROWS, LANES),) * 2,
-        in_specs=[VMEM] * len(offsets),
+        in_specs=[VMEM] * len(offsets) + [ANY] + [VMEM] * 2,
         out_specs=(VMEM, VMEM),
         compiler_params=grant(6),
         name="relay",
-    )(*arrived)
-    ydown, yup, zl, zh = lax.optimization_barrier((ydown, yup, zl, zh))
+    )(*arrived, zdn, zdown, zupper)
     zhup = moved(zl, "group", -1)
     zhdn = moved(zh, "group", 1)
-    y_halos = [moved(yup, "dev", stride), moved(ydown, "dev", -stride)]
-
     wide = pltpu.VMEM((QUADS, EXT * SPAN + 2 * PAD, LANES), jnp.float32)
     by_layer = lambda a: a.reshape(a.shape[:-2] + (SIDE, YQ, LANES))
     sp, wd = by_layer(sp), by_layer(wd)
@@ -799,7 +812,7 @@
         pltpu.VMEM((QUADS, HALF + 2, SPAN, LANES), jnp.float32),
         pltpu.VMEM((FIELDS, QUADS, PLANE // 2, LANES), jnp.float32),
     ]
-    sources = (own, pd, zup, zdn, zhup, zhdn, *y_halos, *z_halos, *arrived)
+    sources = (own, pd, zup, zdn, zhup, zhdn, *arrived)
     ud, fd, *first_half = pl.pallas_call(
         functools.partial(sweep_kernel, pieces),
         out_shape=(f32(QUADS, PLANE, LANES), f32(QUADS, NEAR * SPAN, LANES), *half_out),
@@ -825,16 +838,16 @@
     )(*sources, sp, wd, *scalars)
 
     def second_half():
-        x_halos, x_starts = [], []
-        for sx in (1, -1):
+        halos, starts = [], []
+        for way in ((1, 0), (-1, 0), (0, 1), (0, -1)):
             for k, parts in enumerate(pieces):
                 for name, start in parts:
-                    if name == (sx, 0):
-                        x_halos.append(arrived[k])
-                        x_starts.append(start + Y_ROWS)
-        sources = (own, *x_halos, *y_halos, *z_halos, ud, fd)
+                    if name == way:
+                        halos.append(arrived[k])
+                        starts.append(start + Y_ION)
+        sources = (own, *halos, zhup, zhdn, ud, fd)
         return pl.pallas_call(
-            functools.partial(update_kernel, 1, x_starts),
+            functools.partial(update_kernel, 1, starts),
             out_shape=half_out,
             in_specs=[HBM] * (len(sources) + 2) + [SMEM] * 4,
             out_specs=(VMEM, VMEM),

time: 92.4 us -> 89.4 us (0.968)
  the two profiles are of different devices: /device:TPU:6 before, /device:TPU:16 now
where the time goes in v1:
time: 89.4 us; the launch traced here: 88.7 us
  Pallas kernels  42.8 us (48%)
  waiting for transfers between devices  32.1 us (36%)
  starting transfers between devices  10.9 us (12%)
  between operations  2.21 us (2%)
    pallas_call x1, Pallas kernels, local(): pl.pallas_call(functools.partial(sweep_kernel, pieces), out_shape=(f32(QU...  21.2 us
    ppermute x10, waiting for transfers between devices, moved(): return lax.ppermute(block, axis, [(i, (i + offset) % n) for i in range(n)])  18.8 us
    ppermute x2, waiting for transfers between devices, finished(): lax.ppermute(block, ('group', 'dev'), route)  13.4 us
    ppermute x10, starting transfers between devices, moved(): return lax.ppermute(block, axis, [(i, (i + offset) % n) for i in range(n)])  8.75 us
    pallas_call x1, Pallas kernels, second_half(): pl.pallas_call(functools.partial(update_kernel, 1, starts), out_shape=hal...  7.11 us
    pallas_call x1, Pallas kernels, local(): pl.pallas_call(functools.partial(pack_kernel, pieces), out_shape=(f32(QUA...  6.8 us
    pallas_call x1, Pallas kernels, local(): pl.pallas_call(ions_kernel, out_shape=(f32(PAIRS, QUADS, PLANE, LANES), f...  4.01 us
    ppermute x2, starting transfers between devices, finished(): lax.ppermute(block, ('group', 'dev'), route)  2.16 us
  transfers between devices with their start and end apart: 12, of which 6 were waited for; matrix products, arithmetic and copies ran while one was open for 0% of the time, Pallas kernels for 14%

profile of v1, /device:TPU:16, one launch (start us, length us, event | category | flops | bytes accessed | tf_op | source)
XLA Modules:
  0.0 88.7 jit_solution(751967764681598016)
XLA Ops:
  0.6 6.8 %pack.1 = (f32[4,256,128]{2,1,0:T(8,128)}, f32[8,128]{1,0:T(8,128)S(1)}, f32[496,128]{1,0:T(8,128)}, f32[496,128]{1,0:T(8,128)}, f32[424,128]{1,0:T(8,128)}, /*i...) custom-call(f32[6,512,128]{2,1,0:T(8,128)} %bitcast.98, ...), custom_call_target="tpu_custom_call" | custom-call | tf_op jit(solution)/shard_map/pack/pallas_call | solution.py:749
  7.5 2.5 %collective-permute-start.10 = (f32[360,128]{1,0:T(8,128)}, f32[360,128]{1,0:T(8,128)S(1)}, u32[]{:S(2)}, u32[]{:S(2)}) collective-permute-start(f32[360,128]{1,0:T(8,128)} %get-tuple-element.358), channel_id=1, source_target_pairs={{0,24},{8,0},{16,8},{24,16},{1,25},{9,1},{17,9},{25,17},{2,26},{10... | collective-permute-start | bytes 552968 | tf_op jit(solution)/shard_map/ppermute | solution.py:714
  10.0 0.4 collective-permute-start.14
  10.4 1.7 %collective-permute-start.12 = (f32[496,128]{1,0:T(8,128)}, f32[496,128]{1,0:T(8,128)S(1)}, u32[]{:S(2)}, u32[]{:S(2)}) collective-permute-start(f32[496,128]{1,0:T(8,128)} %get-tuple-element.368), channel_id=1, source_target_pairs={{0,7},{1,0},{2,1},{3,2},{4,3},{5,4},{6,5},{7,6},{8,15},{9,8},{10,9... | collective-permute-start | bytes 761864 | tf_op jit(solution)/shard_map/ppermute | solution.py:714
  12.2 1.9 %collective-permute-start.15 = (f32[72,128]{1,0:T(8,128)}, f32[72,128]{1,0:T(8,128)S(1)}, u32[]{:S(2)}, u32[]{:S(2)}) collective-permute-start(f32[72,128]{1,0:T(8,128)} %get-tuple-element.371), channel_id=1, source_target_pairs={{0,5},{1,6},{2,7},{3,0},{4,1},{5,2},{6,3},{7,4},{8,13},{9,14},{10,... | collective-permute-start | bytes 110600 | tf_op jit(solution)/shard_map/ppermute | solution.py:714
  14.0 4.0 %ions.1 = (f32[3,4,256,128]{3,2,1,0:T(8,128)S(1)}, f32[4,256,128]{2,1,0:T(8,128)S(1)}) custom-call(f32[6,512,128]{2,1,0:T(8,128)} %bitcast.99, s32[512,128]{1,0:T(8,128)} %bitcast.101, f32[512,128]{1,0:T(8,128)} %bitcast.103), custom_call_target="tpu_custom_call" | custom-call | tf_op jit(solution)/shard_map/ions/pallas_call | solution.py:770
  18.0 0.0 collective-permute-done.10.refs_2_
  18.1 0.0 copy-start.16
  18.1 0.0 copy-start.17
  18.1 0.0 copy-start.18
  18.1 0.1 collective-permute-start.13
  18.2 0.6 copy-done.15
  18.7 4.1 %collective-permute-done.15.refs_4_.refs_10_ = f32[72,128]{1,0:T(8,128)S(1)} collective-permute-done((f32[72,128]{1,0:T(8,128)}, f32[72,128]{1,0:T(8,128)S(1)}, u32[]{:S(2)}, u32[]{:S(2)}) %collective-permute-start.15) | collective-permute-done | bytes 36896 | tf_op jit(solution)/shard_map/ppermute | solution.py:714
  22.8 0.0 collective-permute-start.17
  22.9 0.1 collective-permute-start.16
  22.9 1.3 %ion_z_faces.1 = (f32[128,128]{1,0:T(8,128)S(1)}, f32[128,128]{1,0:T(8,128)S(1)}) custom-call(f32[3,4,256,128]{3,2,1,0:T(8,128)S(1)} %get-tuple-element.364.sp, f32[4,256,128]{2,1,0:T(8,128)S(1)} %get-tuple-element.365.wd), custom_call_target="tpu_custom_call" | custom-call | tf_op jit(solution)/shard_map/ion_z_faces/pallas_call | solution.py:784
  24.3 5.5 %collective-permute-done.16.refs_5_.refs_11_ = f32[72,128]{1,0:T(8,128)S(1)} collective-permute-done((f32[72,128]{1,0:T(8,128)S(1)}, f32[72,128]{1,0:T(8,128)S(1)}, u32[]{:S(2)}, u32[]{:S(2)}) %collective-permute-start.16) | collective-permute-done | bytes 36896 | tf_op jit(solution)/shard_map/ppermute | solution.py:714
  29.8 0.0 collective-permute-done.11.refs_1_.refs_7_
  29.8 0.0 copy-start
  29.9 0.3 relay.1
  30.2 0.8 collective-permute-start.18
  31.1 1.3 %collective-permute-start.19 = (f32[416,128]{1,0:T(8,128)S(1)}, f32[416,128]{1,0:T(8,128)}, u32[]{:S(2)}, u32[]{:S(2)}) collective-permute-start(f32[416,128]{1,0:T(8,128)S(1)} %get-tuple-element.377), channel_id=1, source_target_pairs={{0,8},{8,16},{16,24},{24,0},{1,9},{9,17},{17,25},{25,1},{2,10},{10... | collective-permute-start | bytes 638984 | tf_op jit(solution)/shard_map/ppermute | solution.py:714
  33.6 4.5 %collective-permute-done.18.refs_4_ = f32[416,128]{1,0:T(8,128)S(1)} collective-permute-done((f32[416,128]{1,0:T(8,128)S(1)}, f32[416,128]{1,0:T(8,128)S(1)}, u32[]{:S(2)}, u32[]{:S(2)}) %collective-permute-start.18) | collective-permute-done | bytes 213024 | tf_op jit(solution)/shard_map/ppermute | solution.py:714
  38.2 4.6 %collective-permute-done.19.refs_5_ = f32[416,128]{1,0:T(8,128)} collective-permute-done((f32[416,128]{1,0:T(8,128)S(1)}, f32[416,128]{1,0:T(8,128)}, u32[]{:S(2)}, u32[]{:S(2)}) %collective-permute-start.19) | collective-permute-done | bytes 213024 | tf_op jit(solution)/shard_map/ppermute | solution.py:714
  42.8 21.2 %sweeps.1 = (f32[4,256,128]{2,1,0:T(8,128)S(1)}, f32[4,544,128]{2,1,0:T(8,128)S(1)}, f32[7,128,128]{2,1,0:T(8,128)}, f32[7,128,128]{2,1,0:T(8,128)}) custom-call(f32[8,128]{1,0:T(8,128)S(1)} %get-tuple-element.366.refs_0_, f32[4,256,128]{2,1,0:T(8,128)} %get-tuple-element.378.refs_1_, f32[360,128]{1,0:T(8,128)} %copy-done.15, f32[360,128]{1,0:T(8,128)} %copy-done, ...), custom_call_target="tpu_custom_call" | custom-call | tf_op jit(solution)/shard_map/sweeps/pallas_call | solution.py:816
  64.0 24.7 %conditional.1 = (f32[6,2,32768]{2,1,0:T(2,128)}, f32[2,32768]{1,0:T(2,128)}) conditional(s32[]{:T(128)} %clamp.3, (f32[3,4,32,8,128]{4,3,2,1,0:T(8,128)S(1)}, f32[4,32,8,128]{3,2,1,0:T(8,128)S(1)}, f32[8,128]{1,0:T(8,128)S(1)}, f32[496,128]{1,0:T(8,128)}, f32[496,128]{1,0:T(8,128)}, /*index=5*/f32[424,128]{1,0:T(8,128)}, ...), branch_computations={%region_0.1_spmd, %region_1.2_spmd, %region_2.3_spmd, %region_3.4_... | conditional | bytes 5505148 | solution.py:889
  64.1 0.9 collective-permute-start.6
  65.0 7.1 %update.10 = (f32[7,128,128]{2,1,0:T(8,128)S(1)}, f32[7,128,128]{2,1,0:T(8,128)S(1)}) custom-call(f32[3,4,32,8,128]{4,3,2,1,0:T(8,128)S(1)} %get-tuple-element.290.sp, f32[4,32,8,128]{3,2,1,0:T(8,128)S(1)} %get-tuple-element.291.wd, f32[8,128]{1,0:T(8,128)S(1)} %get-tuple-element.292.refs_0_, f32[496,128]{1,0:T(8,128)} %get-tuple-element.293.refs_1_, ...), custom_call_target="tpu_custom_call" | custom-call | tf_op jit(solution)/shard_map/cond/branch_4_fun/update/pallas_call | solution.py:849
  72.1 1.3 %collective-permute-start.7 = (f32[7,128,128]{2,1,0:T(8,128)S(1)}, f32[7,128,128]{2,1,0:T(8,128)S(1)}, u32[]{:S(2)}, u32[]{:S(2)}) collective-permute-start(f32[7,128,128]{2,1,0:T(8,128)S(1)} %get-tuple-element.306), channel_id=1, source_target_pairs={{0,8},{1,9},{2,10},{3,11},{4,12},{5,13},{6,14},{7,15},{8,0},{9,1},... | collective-permute-start | bytes 1376264 | tf_op jit(solution)/shard_map/cond/branch_4_fun/ppermute | solution.py:875
  73.4 4.4 %collective-permute-done.6.refs_2_ = f32[7,128,128]{2,1,0:T(8,128)S(1)} collective-permute-done((f32[7,128,128]{2,1,0:T(8,128)}, f32[7,128,128]{2,1,0:T(8,128)S(1)}, u32[]{:S(2)}, u32[]{:S(2)}) %collective-permute-start.6) | collective-permute-done | bytes 458784 | tf_op jit(solution)/shard_map/cond/branch_4_fun/ppermute | solution.py:875
  77.7 9.0 %collective-permute-done.7.refs_3_ = f32[7,128,128]{2,1,0:T(8,128)S(1)} collective-permute-done((f32[7,128,128]{2,1,0:T(8,128)S(1)}, f32[7,128,128]{2,1,0:T(8,128)S(1)}, u32[]{:S(2)}, u32[]{:S(2)}) %collective-permute-start.7) | collective-permute-done | bytes 458784 | tf_op jit(solution)/shard_map/cond/branch_4_fun/ppermute | solution.py:875
  86.7 2.0 %place.10 = (f32[6,512,128]{2,1,0:T(8,128)}, f32[512,128]{1,0:T(8,128)}) custom-call(s32[1]{0:T(128)} %get-tuple-element.288.refs_12_.give_slot, f32[7,128,128]{2,1,0:T(8,128)S(1)} %copy-done.7, f32[7,128,128]{2,1,0:T(8,128)S(1)} %get-tuple-element.304.refs_1_, f32[7,128,128]{2,1,0:T(8,128)S(1)} %collective-permute-done.6.refs_2_, ...), custom_call_target="tpu_custom_call" | custom-call | tf_op jit(solution)/shard_map/cond/branch_4_fun/place/pallas_call | solution.py:864
  (32 shorter events, 0.1 us)
Async XLA Ops:
  7.4 10.6 %copy-start.19 = (f32[424,128]{1,0:T(8,128)S(1)}, f32[424,128]{1,0:T(8,128)}, u32[]{:S(2)}) copy-start(f32[424,128]{1,0:T(8,128)} %get-tuple-element.369) | copy-start | bytes 651268
  7.5 15.4 %copy-start.20 = (f32[360,128]{1,0:T(8,128)S(1)}, f32[360,128]{1,0:T(8,128)}, u32[]{:S(2)}) copy-start(f32[360,128]{1,0:T(8,128)} %get-tuple-element.373) | copy-start | bytes 552964
  7.5 15.4 %copy-start.21 = (f32[72,128]{1,0:T(8,128)S(1)}, f32[72,128]{1,0:T(8,128)}, u32[]{:S(2)}) copy-start(f32[72,128]{1,0:T(8,128)} %get-tuple-element.372) | copy-start | bytes 110596
  7.5 10.6 %collective-permute-start.10 = (f32[360,128]{1,0:T(8,128)}, f32[360,128]{1,0:T(8,128)S(1)}, u32[]{:S(2)}, u32[]{:S(2)}) collective-permute-start(f32[360,128]{1,0:T(8,128)} %get-tuple-element.358), channel_id=1, source_target_pairs={{0,24},{8,0},{16,8},{24,16},{1,25},{9,1},{17,9},{25,17},{2,26},{10... | collective-permute-start | bytes 552968 | tf_op jit(solution)/shard_map/ppermute | solution.py:714
  10.0 12.9 %collective-permute-start.14 = (f32[424,128]{1,0:T(8,128)}, f32[424,128]{1,0:T(8,128)S(1)}, u32[]{:S(2)}, u32[]{:S(2)}) collective-permute-start(f32[424,128]{1,0:T(8,128)} %get-tuple-element.370), channel_id=1, source_target_pairs={{0,6},{1,7},{2,0},{3,1},{4,2},{5,3},{6,4},{7,5},{8,14},{9,15},{10,... | collective-permute-start | bytes 651272 | tf_op jit(solution)/shard_map/ppermute | solution.py:714
  10.4 19.4 %collective-permute-start.11 = (f32[496,128]{1,0:T(8,128)}, f32[496,128]{1,0:T(8,128)S(1)}, u32[]{:S(2)}, u32[]{:S(2)}) collective-permute-start(f32[496,128]{1,0:T(8,128)} %get-tuple-element.367), channel_id=1, source_target_pairs={{0,1},{1,2},{2,3},{3,4},{4,5},{5,6},{6,7},{7,0},{8,9},{9,10},{10,1... | collective-permute-start | bytes 761864 | tf_op jit(solution)/shard_map/ppermute | solution.py:714
  10.4 19.4 %collective-permute-start.12 = (f32[496,128]{1,0:T(8,128)}, f32[496,128]{1,0:T(8,128)S(1)}, u32[]{:S(2)}, u32[]{:S(2)}) collective-permute-start(f32[496,128]{1,0:T(8,128)} %get-tuple-element.368), channel_id=1, source_target_pairs={{0,7},{1,0},{2,1},{3,2},{4,3},{5,4},{6,5},{7,6},{8,15},{9,8},{10,9... | collective-permute-start | bytes 761864 | tf_op jit(solution)/shard_map/ppermute | solution.py:714
  12.2 10.7 %collective-permute-start.15 = (f32[72,128]{1,0:T(8,128)}, f32[72,128]{1,0:T(8,128)S(1)}, u32[]{:S(2)}, u32[]{:S(2)}) collective-permute-start(f32[72,128]{1,0:T(8,128)} %get-tuple-element.371), channel_id=1, source_target_pairs={{0,5},{1,6},{2,7},{3,0},{4,1},{5,2},{6,3},{7,4},{8,13},{9,14},{10,... | collective-permute-start | bytes 110600 | tf_op jit(solution)/shard_map/ppermute | solution.py:714
  18.1 0.7 copy-start.15
  18.1 24.7 %copy-start.16 = (f32[6]{0:T(128)S(1)}, f32[6]{0:T(128)}, u32[]{:S(2)}) copy-start(f32[6]{0:T(128)} %refs_14_.1) | copy-start | bytes 76
  18.1 24.7 %copy-start.17 = (f32[2]{0:T(128)S(1)}, f32[2]{0:T(128)}, u32[]{:S(2)}) copy-start(f32[2]{0:T(128)} %refs_15_.1) | copy-start | bytes 28
  18.1 24.7 %copy-start.18 = (s32[2]{0:T(128)S(1)}, s32[2]{0:T(128)}, u32[]{:S(2)}) copy-start(s32[2]{0:T(128)} %refs_16_.1) | copy-start | bytes 28
  18.1 11.7 %collective-permute-start.13 = (f32[424,128]{1,0:T(8,128)S(1)}, f32[424,128]{1,0:T(8,128)S(1)}, u32[]{:S(2)}, u32[]{:S(2)}) collective-permute-start(f32[424,128]{1,0:T(8,128)S(1)} %copy-done.19), channel_id=1, source_target_pairs={{0,2},{1,3},{2,4},{3,5},{4,6},{5,7},{6,0},{7,1},{8,10},{9,11},{10,... | collective-permute-start | bytes 651272 | tf_op jit(solution)/shard_map/ppermute | solution.py:714
  22.8 7.4 %copy-start.1 = (f32[72,128]{1,0:T(8,128)}, f32[72,128]{1,0:T(8,128)S(1)}, u32[]{:S(2)}) copy-start(f32[72,128]{1,0:T(8,128)S(1)} %collective-permute-done.15.refs_4_.refs_10_) | copy-start | bytes 110596
  22.8 7.0 %collective-permute-start.17 = (f32[360,128]{1,0:T(8,128)S(1)}, f32[360,128]{1,0:T(8,128)S(1)}, u32[]{:S(2)}, u32[]{:S(2)}) collective-permute-start(f32[360,128]{1,0:T(8,128)S(1)} %copy-done.20), channel_id=1, source_target_pairs={{0,8},{8,16},{16,24},{24,0},{1,9},{9,17},{17,25},{25,1},{2,10},{10... | collective-permute-start | bytes 552968 | tf_op jit(solution)/shard_map/ppermute | solution.py:714
  22.9 7.4 %copy-start.11 = (f32[424,128]{1,0:T(8,128)}, f32[424,128]{1,0:T(8,128)S(1)}, u32[]{:S(2)}) copy-start(f32[424,128]{1,0:T(8,128)S(1)} %collective-permute-done.14.refs_2_.refs_8_) | copy-start | bytes 651268
  22.9 6.9 %collective-permute-start.16 = (f32[72,128]{1,0:T(8,128)S(1)}, f32[72,128]{1,0:T(8,128)S(1)}, u32[]{:S(2)}, u32[]{:S(2)}) collective-permute-start(f32[72,128]{1,0:T(8,128)S(1)} %copy-done.21), channel_id=1, source_target_pairs={{0,3},{1,4},{2,5},{3,6},{4,7},{5,0},{6,1},{7,2},{8,11},{9,12},{10,... | collective-permute-start | bytes 110600 | tf_op jit(solution)/shard_map/ppermute | solution.py:714
  29.8 13.0 %copy-start.2 = (f32[72,128]{1,0:T(8,128)}, f32[72,128]{1,0:T(8,128)S(1)}, u32[]{:S(2)}) copy-start(f32[72,128]{1,0:T(8,128)S(1)} %collective-permute-done.16.refs_5_.refs_11_) | copy-start | bytes 110596
  29.8 2.5 %copy-start.9 = (f32[496,128]{1,0:T(8,128)}, f32[496,128]{1,0:T(8,128)S(1)}, u32[]{:S(2)}) copy-start(f32[496,128]{1,0:T(8,128)S(1)} %collective-permute-done.11.refs_1_.refs_7_) | copy-start | bytes 761860
  29.8 13.0 %copy-start.10 = (f32[496,128]{1,0:T(8,128)}, f32[496,128]{1,0:T(8,128)S(1)}, u32[]{:S(2)}) copy-start(f32[496,128]{1,0:T(8,128)S(1)} %collective-permute-done.12.refs_0_.refs_6_) | copy-start | bytes 761860
  29.8 13.0 %copy-start = (f32[360,128]{1,0:T(8,128)}, f32[360,128]{1,0:T(8,128)S(1)}, u32[]{:S(2)}) copy-start(f32[360,128]{1,0:T(8,128)S(1)} %collective-permute-done.17.refs_6_.refs_3_) | copy-start | bytes 552964
  29.9 2.5 %copy-start.12 = (f32[424,128]{1,0:T(8,128)}, f32[424,128]{1,0:T(8,128)S(1)}, u32[]{:S(2)}) copy-start(f32[424,128]{1,0:T(8,128)S(1)} %collective-permute-done.13.refs_3_.refs_9_) | copy-start | bytes 651268
  30.2 7.9 %collective-permute-start.18 = (f32[416,128]{1,0:T(8,128)S(1)}, f32[416,128]{1,0:T(8,128)S(1)}, u32[]{:S(2)}, u32[]{:S(2)}) collective-permute-start(f32[416,128]{1,0:T(8,128)S(1)} %get-tuple-element.376), channel_id=1, source_target_pairs={{0,24},{8,0},{16,8},{24,16},{1,25},{9,1},{17,9},{25,17},{2,26},{10... | collective-permute-start | bytes 638984 | tf_op jit(solution)/shard_map/ppermute | solution.py:714
  31.1 11.7 %collective-permute-start.19 = (f32[416,128]{1,0:T(8,128)S(1)}, f32[416,128]{1,0:T(8,128)}, u32[]{:S(2)}, u32[]{:S(2)}) collective-permute-start(f32[416,128]{1,0:T(8,128)S(1)} %get-tuple-element.377), channel_id=1, source_target_pairs={{0,8},{8,16},{16,24},{24,0},{1,9},{9,17},{17,25},{25,1},{2,10},{10... | collective-permute-start | bytes 638984 | tf_op jit(solution)/shard_map/ppermute | solution.py:714
  38.2 4.6 %copy-start.13 = (f32[416,128]{1,0:T(8,128)}, f32[416,128]{1,0:T(8,128)S(1)}, u32[]{:S(2)}) copy-start(f32[416,128]{1,0:T(8,128)S(1)} %collective-permute-done.18.refs_4_) | copy-start | bytes 638980
  64.1 13.6 %collective-permute-start.6 = (f32[7,128,128]{2,1,0:T(8,128)}, f32[7,128,128]{2,1,0:T(8,128)S(1)}, u32[]{:S(2)}, u32[]{:S(2)}) collective-permute-start(f32[7,128,128]{2,1,0:T(8,128)} %get-tuple-element.305), channel_id=1, source_target_pairs={{0,8},{1,9},{2,10},{3,11},{4,12},{5,13},{6,14},{7,15},{8,0},{9,1},... | collective-permute-start | bytes 1376264 | tf_op jit(solution)/shard_map/cond/branch_4_fun/ppermute | solution.py:875
  65.0 21.8 %copy-start.7 = (f32[7,128,128]{2,1,0:T(8,128)S(1)}, f32[7,128,128]{2,1,0:T(8,128)}, u32[]{:S(2)}) copy-start(f32[7,128,128]{2,1,0:T(8,128)} %get-tuple-element.289.refs_0_) | copy-start | bytes 1376260 | tf_op jit(solution)/shard_map/cond
  72.1 14.7 %collective-permute-start.7 = (f32[7,128,128]{2,1,0:T(8,128)S(1)}, f32[7,128,128]{2,1,0:T(8,128)S(1)}, u32[]{:S(2)}, u32[]{:S(2)}) collective-permute-start(f32[7,128,128]{2,1,0:T(8,128)S(1)} %get-tuple-element.306), channel_id=1, source_target_pairs={{0,8},{1,9},{2,10},{3,11},{4,12},{5,13},{6,14},{7,15},{8,0},{9,1},... | collective-permute-start | bytes 1376264 | tf_op jit(solution)/shard_map/cond/branch_4_fun/ppermute | solution.py:875

commit v2 on v1

--- a/solution.py
+++ b/solution.py
@@ -51,7 +51,7 @@
 CORNERS = ((-1, -1), (-1, 1), (1, -1), (1, 1))
 SPAN = 16
 EXT = SIDE + 2 * DEPTH
-MIDDLE = 10
+MIDDLE = 15
 PARTS = 3
 PART = 4
 NEAR = SIDE + 2
@@ -161,7 +161,7 @@
         for c in parts[part]:
             c.wait()
         end = min((part + 1) * PART, THIRD - 1)
-        lax.fori_loop(part * PART, end, lambda i, carry: (step(i), carry)[1], 0)
+        lax.fori_loop(part * PART, end, lambda i, carry: (step(i), carry)[1], 0, unroll=True)
     step(THIRD - 1, 2)
 
     zlo[ZC_TBL:, :] = table
@@ -327,7 +327,49 @@
     core = (lane64 >= 16) & (lane64 < 48)
     upper = lane64 >= 48
 
-    for c in copies:
+    for c in copies[:4]:
+        c.wait()
+    def sign(held, way):
+        return jnp.broadcast_to(held[way : way + 1, :], (8, LANES))
+
+    outer = {}
+
+    def outward(key, held):
+        m = jnp.where(upper, sign(held, 4), sign(held, 5))
+        outer[key] = jnp.where(low, 1.0, m)
+
+    outward((0, 0), own)
+
+    def spread(v, zu, zd, shift_u, shift_d, key):
+        rows = v.shape[0]
+        tall = lambda a: a if rows == 8 else jnp.concatenate([a] * (rows // 8), axis=0)
+        if zu is None:
+            return roll(v, 16), roll(v, -16)
+        m, c, u = tall(outer[key]), tall(core), tall(upper)
+        pot = jnp.where(u, roll(zu, 48 + shift_u), roll(zd, -16 + shift_d)) * m
+        rho = jnp.where(u, roll(zu, 16 + shift_u), roll(zd, -48 + shift_d)) * m
+        return jnp.where(c, roll(v, 16), pot), jnp.where(c, roll(v, -16), rho)
+
+    def fill(i, c):
+        x = i + c * THIRD
+        at = pl.ds(pl.multiple_of(x * 8, 8), 8)
+        to = pl.ds(pl.multiple_of(PAD + (x + DEPTH) * SPAN + 4, 4), 8)
+        for j in range(QUADS):
+            zat = pl.ds(pl.multiple_of((j * THIRD + i) * 8, 8), 8)
+            pot, rho = spread(pd[j, at, :], zup[zat, :], zdn[zat, :], -DEPTH * c, DEPTH * c, (0, 0))
+            ua[j, to, :] = pot
+            dn[j, to, :] = rho
+
+    def fill_three(i, carry):
+        for c in range(3):
+            fill(i, c)
+        return carry
+
+    lax.fori_loop(0, THIRD - 1, fill_three, 0, unroll=2)
+    fill(THIRD - 1, 0)
+    fill(THIRD - 1, 1)
+
+    for c in copies[4:]:
         c.wait()
     table = {(0, 0): own[...]}
     ztable = {1: {(0, 0): zup[ZC_TBL:, :]}, -1: {(0, 0): zdn[ZC_TBL:, :]}}
@@ -340,9 +382,6 @@
         ref, base = where[(-sx, -sy)]
         table[(sx, sy)] = ref[base + EDGE_TBL : base + EDGE_ROWS, :]
 
-    def sign(held, way):
-        return jnp.broadcast_to(held[way : way + 1, :], (8, LANES))
-
     def crossing(way, here, there):
         level = sign(table[here], way)
         beyond = {}
@@ -351,6 +390,9 @@
             beyond[sz] = sign(ztable[sz][here], way) * sign(table[here], z) * sign(table[there], z)
         m = jnp.where(core, level, jnp.where(upper, beyond[1], beyond[-1]))
         return jnp.where(low, 1.0, m)
+
+    for key, held_table in table.items():
+        outward(key, held_table)
 
     row8 = lax.broadcasted_iota(jnp.int32, (8, LANES), 0)
     one = jnp.ones((8, LANES), jnp.float32)
@@ -366,40 +408,6 @@
         myp[number, 8:16, :] = jnp.where(row8 == 3, m[1], one)
         mym[number, 0:8, :] = jnp.where(row8 == 4, m[-1], one)
         mym[number, 8:16, :] = jnp.where(row8 == 4, m[1], one)
-
-    outer = {}
-    for key, held in table.items():
-        m = jnp.where(upper, sign(held, 4), sign(held, 5))
-        outer[key] = jnp.where(low, 1.0, m)
-
-    def spread(v, zu, zd, shift_u, shift_d, key):
-        rows = v.shape[0]
-        tall = lambda a: a if rows == 8 else jnp.concatenate([a] * (rows // 8), axis=0)
-        if zu is None:
-            return roll(v, 16), roll(v, -16)
-        m, c, u = tall(outer[key]), tall(core), tall(upper)
-        pot = jnp.where(u, roll(zu, 48 + shift_u), roll(zd, -16 + shift_d)) * m
-        rho = jnp.where(u, roll(zu, 16 + shift_u), roll(zd, -48 + shift_d)) * m
-        return jnp.where(c, roll(v, 16), pot), jnp.where(c, roll(v, -16), rho)
-
-    def fill(i, c):
-        x = i + c * THIRD
-        at = pl.ds(pl.multiple_of(x * 8, 8), 8)
-        to = pl.ds(pl.multiple_of(PAD + (x + DEPTH) * SPAN + 4, 4), 8)
-        for j in range(QUADS):
-            zat = pl.ds(pl.multiple_of((j * THIRD + i) * 8, 8), 8)
-            pot, rho = spread(pd[j, at, :], zup[zat, :], zdn[zat, :], -DEPTH * c, DEPTH * c, (0, 0))
-            ua[j, to, :] = pot
-            dn[j, to, :] = rho
-
-    def fill_three(i, carry):
-        for c in range(3):
-            fill(i, c)
-        return carry
-
-    lax.fori_loop(0, THIRD - 1, fill_three, 0)
-    fill(THIRD - 1, 0)
-    fill(THIRD - 1, 1)
 
     for number, (sx, sy) in enumerate(SIDES):
         ref, base = where[(-sx, -sy)]
@@ -440,7 +448,8 @@
     scale = 1.0 / (6.0 + screening)
 
     def slab(src, dst, x, sx, before=None, after=None):
-        r = pl.multiple_of(PAD + (x + DEPTH) * SPAN, 8)
+        r = PAD + (x + DEPTH) * SPAN
+        r = r if isinstance(x, int) else pl.multiple_of(r, 8)
         at = pl.ds(r, SPAN)
         c = [src[j, at, :] for j in range(QUADS)]
         for j in range(QUADS):
@@ -461,48 +470,49 @@
                 slab(src, dst, 1 + i * MIDDLE + n, 0)
             return carry
 
-        def fringe(i, carry):
-            for n in range(2):
-                slab(src, dst, -2 - 2 * i - n, -1)
-                slab(src, dst, SIDE + 1 + 2 * i + n, 1)
-            return carry
-
         lax.fori_loop(0, (SIDE - 2) // MIDDLE, middle, 0)
         slab(src, dst, -1, -1, after=0)
         slab(src, dst, 0, 0, before=0)
         slab(src, dst, SIDE - 1, 0, after=1)
         slab(src, dst, SIDE, 1, before=1)
-        lax.fori_loop(0, (SWEEPS + 1 - t) // 2, fringe, 0)
-
-    def two_sweeps(i, carry):
-        sweep(ua, ub, 2 * i + 1)
-        sweep(ub, ua, 2 * i + 2)
-        return carry
-
-    lax.fori_loop(0, SWEEPS // 2, two_sweeps, 0)
+        for n in range(DEPTH - t - 1):
+            slab(src, dst, -2 - n, -1)
+            slab(src, dst, SIDE + 1 + n, 1)
+
+    for t in range(1, SWEEPS + 1):
+        sweep(*((ua, ub) if t % 2 else (ub, ua)), t)
 
     lane16 = lane_of(SPAN)
     first = (lane16 & 32) == 0
     row16 = lax.broadcasted_iota(jnp.int32, (SPAN, LANES), 0)
 
-    def slots(x, m, centre=False):
-        r = pl.multiple_of(PAD + (x + DEPTH) * SPAN, 8)
-        near = pl.ds(pl.multiple_of((x + 1) * SPAN, 8), SPAN)
+    def slots(v, m):
+        wide_lane = lane_of(v.shape[0])
+        c = v * m
+        r = roll(c, 64)
+        u = 0.5 * jnp.where(wide_lane < 64, c + r, r - c)
+        return u, jnp.where((wide_lane & 32) == 0, roll(u, -16), roll(u, 16))
+
+    def rows_at(x):
+        return pl.ds(PAD + (x + DEPTH) * SPAN + 4, 8), pl.ds((x + 1) * SPAN + 4, 8)
+
+    for x, number in ((-1, 0), (SIDE, 1)):
+        at, near = rows_at(x)
         for j in range(QUADS):
-            c = ua[j, pl.ds(r, SPAN), :] * m
-            t = roll(c, 64)
-            u = 0.5 * jnp.where(lane16 < 64, c + t, t - c)
-            if centre:
-                udv[j, pl.ds(pl.multiple_of(x * 8, 8), 8), :] = u[4:12]
-            fdv[j, near, :] = jnp.where(first, roll(u, -16), roll(u, 16))
-
-    tall = lambda a: jnp.concatenate([a, a], axis=0)
-    beside = jnp.where(row16 >= 12, tall(y_sign[0][1]), jnp.where(row16 < 4, tall(y_sign[0][-1]), 1.0))
-    slots(-1, mx[0])
-    slots(SIDE, mx[1])
+            fdv[j, near, :] = slots(ua[j, at, :], mx[number, 4:12, :])[1]
+    for j, row, sy in ((0, 12, 1), (3, 3, -1)):
+        v = ua[j, pl.ds(PAD + DEPTH * SPAN + row, SIDE, stride=SPAN), :]
+        m = jnp.concatenate([y_sign[0][sy]] * (SIDE // 8), axis=0)
+        fdv[j, pl.ds(SPAN + row, SIDE, stride=SPAN), :] = slots(v, m)[1]
+
     def all_slots(i, carry):
         for n in range(4):
-            slots(4 * i + n, beside, True)
+            x = 4 * i + n
+            at, near = rows_at(x)
+            for j in range(QUADS):
+                u, dense = slots(ua[j, at, :], one)
+                udv[j, pl.ds(pl.multiple_of(x * 8, 8), 8), :] = u
+                fdv[j, near, :] = dense
         return carry
 
     lax.fori_loop(0, SIDE // 4, all_slots, 0)

time: 89.4 us -> 84.8 us (0.949)
  the two profiles are of different devices: /device:TPU:16 before, /device:TPU:6 now
where the time goes in v2:
time: 84.8 us; the launch traced here: 83.4 us
  Pallas kernels  38.1 us (45%)
  waiting for transfers between devices  26 us (31%)
  starting transfers between devices  16.8 us (20%)
  between operations  2.17 us (3%)
    pallas_call x1, Pallas kernels, local(): pl.pallas_call(functools.partial(sweep_kernel, pieces), out_shape=(f32(QU...  18.4 us
    ppermute x10, starting transfers between devices, moved(): return lax.ppermute(block, axis, [(i, (i + offset) % n) for i in range(n)])  13.8 us
    ppermute x10, waiting for transfers between devices, moved(): return lax.ppermute(block, axis, [(i, (i + offset) % n) for i in range(n)])  13.4 us
    ppermute x2, waiting for transfers between devices, finished(): lax.ppermute(block, ('group', 'dev'), route)  12.5 us
    pallas_call x1, Pallas kernels, second_half(): pl.pallas_call(functools.partial(update_kernel, 1, starts), out_shape=hal...  7.11 us
    pallas_call x1, Pallas kernels, local(): pl.pallas_call(functools.partial(pack_kernel, pieces), out_shape=(f32(QUA...  4.99 us
    pallas_call x1, Pallas kernels, local(): pl.pallas_call(ions_kernel, out_shape=(f32(PAIRS, QUADS, PLANE, LANES), f...  4.01 us
    ppermute x2, starting transfers between devices, finished(): lax.ppermute(block, ('group', 'dev'), route)  3.06 us
  transfers between devices with their start and end apart: 12, of which 6 were waited for; matrix products, arithmetic and copies ran while one was open for 0% of the time, Pallas kernels for 15%

profile of v2, /device:TPU:6, one launch (start us, length us, event | category | flops | bytes accessed | tf_op | source)
XLA Modules:
  0.0 83.4 jit_solution(14308954560609567319)
XLA Ops:
  0.6 5.0 %pack.1 = (f32[4,256,128]{2,1,0:T(8,128)}, f32[8,128]{1,0:T(8,128)S(1)}, f32[496,128]{1,0:T(8,128)}, f32[496,128]{1,0:T(8,128)}, f32[424,128]{1,0:T(8,128)}, /*i...) custom-call(f32[6,512,128]{2,1,0:T(8,128)} %bitcast.98, ...), custom_call_target="tpu_custom_call" | custom-call | tf_op jit(solution)/shard_map/pack/pallas_call | solution.py:759
  5.7 0.6 collective-permute-start.10
  6.2 3.6 %collective-permute-start.14 = (f32[424,128]{1,0:T(8,128)}, f32[424,128]{1,0:T(8,128)S(1)}, u32[]{:S(2)}, u32[]{:S(2)}) collective-permute-start(f32[424,128]{1,0:T(8,128)} %get-tuple-element.370), channel_id=1, source_target_pairs={{0,6},{1,7},{2,0},{3,1},{4,2},{5,3},{6,4},{7,5},{8,14},{9,15},{10,... | collective-permute-start | bytes 651272 | tf_op jit(solution)/shard_map/ppermute | solution.py:724
  9.8 0.0 collective-permute-start.11
  9.8 3.5 %collective-permute-start.12 = (f32[496,128]{1,0:T(8,128)}, f32[496,128]{1,0:T(8,128)S(1)}, u32[]{:S(2)}, u32[]{:S(2)}) collective-permute-start(f32[496,128]{1,0:T(8,128)} %get-tuple-element.368), channel_id=1, source_target_pairs={{0,7},{1,0},{2,1},{3,2},{4,3},{5,4},{6,5},{7,6},{8,15},{9,8},{10,9... | collective-permute-start | bytes 761864 | tf_op jit(solution)/shard_map/ppermute | solution.py:724
  13.4 0.0 collective-permute-start.15
  13.4 4.0 %ions.1 = (f32[3,4,256,128]{3,2,1,0:T(8,128)S(1)}, f32[4,256,128]{2,1,0:T(8,128)S(1)}) custom-call(f32[6,512,128]{2,1,0:T(8,128)} %bitcast.99, s32[512,128]{1,0:T(8,128)} %bitcast.101, f32[512,128]{1,0:T(8,128)} %bitcast.103), custom_call_target="tpu_custom_call" | custom-call | tf_op jit(solution)/shard_map/ions/pallas_call | solution.py:780
  17.4 0.0 collective-permute-done.10.refs_2_
  17.4 0.0 copy-start.16
  17.5 0.0 copy-start.17
  17.5 0.0 copy-start.18
  17.5 0.6 collective-permute-start.13
  18.1 0.0 copy-done.15
  18.1 3.5 %collective-permute-done.15.refs_4_.refs_10_ = f32[72,128]{1,0:T(8,128)S(1)} collective-permute-done((f32[72,128]{1,0:T(8,128)}, f32[72,128]{1,0:T(8,128)S(1)}, u32[]{:S(2)}, u32[]{:S(2)}) %collective-permute-start.15) | collective-permute-done | bytes 36896 | tf_op jit(solution)/shard_map/ppermute | solution.py:724
  21.6 2.4 %collective-permute-start.17 = (f32[360,128]{1,0:T(8,128)S(1)}, f32[360,128]{1,0:T(8,128)S(1)}, u32[]{:S(2)}, u32[]{:S(2)}) collective-permute-start(f32[360,128]{1,0:T(8,128)S(1)} %copy-done.20), channel_id=1, source_target_pairs={{0,8},{8,16},{16,24},{24,0},{1,9},{9,17},{17,25},{25,1},{2,10},{10... | collective-permute-start | bytes 552968 | tf_op jit(solution)/shard_map/ppermute | solution.py:724
  24.0 0.1 collective-permute-start.16
  24.0 1.3 %ion_z_faces.1 = (f32[128,128]{1,0:T(8,128)S(1)}, f32[128,128]{1,0:T(8,128)S(1)}) custom-call(f32[3,4,256,128]{3,2,1,0:T(8,128)S(1)} %get-tuple-element.364.sp, f32[4,256,128]{2,1,0:T(8,128)S(1)} %get-tuple-element.365.wd), custom_call_target="tpu_custom_call" | custom-call | tf_op jit(solution)/shard_map/ion_z_faces/pallas_call | solution.py:794
  25.4 3.0 %collective-permute-done.16.refs_5_.refs_11_ = f32[72,128]{1,0:T(8,128)S(1)} collective-permute-done((f32[72,128]{1,0:T(8,128)S(1)}, f32[72,128]{1,0:T(8,128)S(1)}, u32[]{:S(2)}, u32[]{:S(2)}) %collective-permute-start.16) | collective-permute-done | bytes 36896 | tf_op jit(solution)/shard_map/ppermute | solution.py:724
  28.4 0.0 copy-start
  28.5 0.3 relay.1
  28.8 1.0 %collective-permute-start.18 = (f32[416,128]{1,0:T(8,128)S(1)}, f32[416,128]{1,0:T(8,128)S(1)}, u32[]{:S(2)}, u32[]{:S(2)}) collective-permute-start(f32[416,128]{1,0:T(8,128)S(1)} %get-tuple-element.376), channel_id=1, source_target_pairs={{0,24},{8,0},{16,8},{24,16},{1,25},{9,1},{17,9},{25,17},{2,26},{10... | collective-permute-start | bytes 638984 | tf_op jit(solution)/shard_map/ppermute | solution.py:724
  29.9 1.9 %collective-permute-start.19 = (f32[416,128]{1,0:T(8,128)S(1)}, f32[416,128]{1,0:T(8,128)}, u32[]{:S(2)}, u32[]{:S(2)}) collective-permute-start(f32[416,128]{1,0:T(8,128)S(1)} %get-tuple-element.377), channel_id=1, source_target_pairs={{0,8},{8,16},{16,24},{24,0},{1,9},{9,17},{17,25},{25,1},{2,10},{10... | collective-permute-start | bytes 638984 | tf_op jit(solution)/shard_map/ppermute | solution.py:724
  33.1 4.8 %collective-permute-done.18.refs_4_ = f32[416,128]{1,0:T(8,128)S(1)} collective-permute-done((f32[416,128]{1,0:T(8,128)S(1)}, f32[416,128]{1,0:T(8,128)S(1)}, u32[]{:S(2)}, u32[]{:S(2)}) %collective-permute-start.18) | collective-permute-done | bytes 213024 | tf_op jit(solution)/shard_map/ppermute | solution.py:724
  38.0 2.1 %collective-permute-done.19.refs_5_ = f32[416,128]{1,0:T(8,128)} collective-permute-done((f32[416,128]{1,0:T(8,128)S(1)}, f32[416,128]{1,0:T(8,128)}, u32[]{:S(2)}, u32[]{:S(2)}) %collective-permute-start.19) | collective-permute-done | bytes 213024 | tf_op jit(solution)/shard_map/ppermute | solution.py:724
  40.1 18.4 %sweeps.1 = (f32[4,256,128]{2,1,0:T(8,128)S(1)}, f32[4,544,128]{2,1,0:T(8,128)S(1)}, f32[7,128,128]{2,1,0:T(8,128)}, f32[7,128,128]{2,1,0:T(8,128)}) custom-call(f32[8,128]{1,0:T(8,128)S(1)} %get-tuple-element.366.refs_0_, f32[4,256,128]{2,1,0:T(8,128)} %get-tuple-element.378.refs_1_, f32[360,128]{1,0:T(8,128)} %copy-done.15, f32[360,128]{1,0:T(8,128)} %copy-done, ...), custom_call_target="tpu_custom_call" | custom-call | tf_op jit(solution)/shard_map/sweeps/pallas_call | solution.py:826
  58.5 24.9 %conditional.1 = (f32[6,2,32768]{2,1,0:T(2,128)}, f32[2,32768]{1,0:T(2,128)}) conditional(s32[]{:T(128)} %clamp.3, (f32[3,4,32,8,128]{4,3,2,1,0:T(8,128)S(1)}, f32[4,32,8,128]{3,2,1,0:T(8,128)S(1)}, f32[8,128]{1,0:T(8,128)S(1)}, f32[496,128]{1,0:T(8,128)}, f32[496,128]{1,0:T(8,128)}, /*index=5*/f32[424,128]{1,0:T(8,128)}, ...), branch_computations={%region_0.1_spmd, %region_1.2_spmd, %region_2.3_spmd, %region_3.4_... | conditional | bytes 5505148 | solution.py:899
  58.7 1.8 %collective-permute-start.4 = (f32[7,128,128]{2,1,0:T(8,128)}, f32[7,128,128]{2,1,0:T(8,128)S(1)}, u32[]{:S(2)}, u32[]{:S(2)}) collective-permute-start(f32[7,128,128]{2,1,0:T(8,128)} %get-tuple-element.284), channel_id=1, source_target_pairs={{0,4},{1,5},{2,6},{3,7},{4,0},{5,1},{6,2},{7,3},{8,12},{9,13},{10,... | collective-permute-start | bytes 1376264 | tf_op jit(solution)/shard_map/cond/branch_3_fun/ppermute | solution.py:885
  60.5 7.1 %update.9 = (f32[7,128,128]{2,1,0:T(8,128)S(1)}, f32[7,128,128]{2,1,0:T(8,128)S(1)}) custom-call(f32[3,4,32,8,128]{4,3,2,1,0:T(8,128)S(1)} %get-tuple-element.269.sp, f32[4,32,8,128]{3,2,1,0:T(8,128)S(1)} %get-tuple-element.270.wd, f32[8,128]{1,0:T(8,128)S(1)} %get-tuple-element.271.refs_0_, f32[496,128]{1,0:T(8,128)} %get-tuple-element.272.refs_1_, ...), custom_call_target="tpu_custom_call" | custom-call | tf_op jit(solution)/shard_map/cond/branch_3_fun/update/pallas_call | solution.py:859
  67.7 1.2 %collective-permute-start.5 = (f32[7,128,128]{2,1,0:T(8,128)S(1)}, f32[7,128,128]{2,1,0:T(8,128)S(1)}, u32[]{:S(2)}, u32[]{:S(2)}) collective-permute-start(f32[7,128,128]{2,1,0:T(8,128)S(1)} %get-tuple-element.285), channel_id=1, source_target_pairs={{0,4},{1,5},{2,6},{3,7},{4,0},{5,1},{6,2},{7,3},{8,12},{9,13},{10,... | collective-permute-start | bytes 1376264 | tf_op jit(solution)/shard_map/cond/branch_3_fun/ppermute | solution.py:885
  68.9 3.1 %collective-permute-done.4.refs_2_ = f32[7,128,128]{2,1,0:T(8,128)S(1)} collective-permute-done((f32[7,128,128]{2,1,0:T(8,128)}, f32[7,128,128]{2,1,0:T(8,128)S(1)}, u32[]{:S(2)}, u32[]{:S(2)}) %collective-permute-start.4) | collective-permute-done | bytes 458784 | tf_op jit(solution)/shard_map/cond/branch_3_fun/ppermute | solution.py:885
  72.0 9.4 %collective-permute-done.5.refs_3_ = f32[7,128,128]{2,1,0:T(8,128)S(1)} collective-permute-done((f32[7,128,128]{2,1,0:T(8,128)S(1)}, f32[7,128,128]{2,1,0:T(8,128)S(1)}, u32[]{:S(2)}, u32[]{:S(2)}) %collective-permute-start.5) | collective-permute-done | bytes 458784 | tf_op jit(solution)/shard_map/cond/branch_3_fun/ppermute | solution.py:885
  81.4 2.0 %place.9 = (f32[6,512,128]{2,1,0:T(8,128)}, f32[512,128]{1,0:T(8,128)}) custom-call(s32[1]{0:T(128)} %get-tuple-element.267.refs_12_.give_slot, f32[7,128,128]{2,1,0:T(8,128)S(1)} %copy-done.6, f32[7,128,128]{2,1,0:T(8,128)S(1)} %get-tuple-element.283.refs_1_, f32[7,128,128]{2,1,0:T(8,128)S(1)} %collective-permute-done.4.refs_2_, ...), custom_call_target="tpu_custom_call" | custom-call | tf_op jit(solution)/shard_map/cond/branch_3_fun/place/pallas_call | solution.py:874
  (32 shorter events, 0.1 us)
Async XLA Ops:
  5.6 11.8 %copy-start.19 = (f32[424,128]{1,0:T(8,128)S(1)}, f32[424,128]{1,0:T(8,128)}, u32[]{:S(2)}) copy-start(f32[424,128]{1,0:T(8,128)} %get-tuple-element.369) | copy-start | bytes 651268
  5.6 15.9 %copy-start.20 = (f32[360,128]{1,0:T(8,128)S(1)}, f32[360,128]{1,0:T(8,128)}, u32[]{:S(2)}) copy-start(f32[360,128]{1,0:T(8,128)} %get-tuple-element.373) | copy-start | bytes 552964
  5.6 18.3 %copy-start.21 = (f32[72,128]{1,0:T(8,128)S(1)}, f32[72,128]{1,0:T(8,128)}, u32[]{:S(2)}) copy-start(f32[72,128]{1,0:T(8,128)} %get-tuple-element.372) | copy-start | bytes 110596
  5.7 11.8 %collective-permute-start.10 = (f32[360,128]{1,0:T(8,128)}, f32[360,128]{1,0:T(8,128)S(1)}, u32[]{:S(2)}, u32[]{:S(2)}) collective-permute-start(f32[360,128]{1,0:T(8,128)} %get-tuple-element.358), channel_id=1, source_target_pairs={{0,24},{8,0},{16,8},{24,16},{1,25},{9,1},{17,9},{25,17},{2,26},{10... | collective-permute-start | bytes 552968 | tf_op jit(solution)/shard_map/ppermute | solution.py:724
  6.2 17.7 %collective-permute-start.14 = (f32[424,128]{1,0:T(8,128)}, f32[424,128]{1,0:T(8,128)S(1)}, u32[]{:S(2)}, u32[]{:S(2)}) collective-permute-start(f32[424,128]{1,0:T(8,128)} %get-tuple-element.370), channel_id=1, source_target_pairs={{0,6},{1,7},{2,0},{3,1},{4,2},{5,3},{6,4},{7,5},{8,14},{9,15},{10,... | collective-permute-start | bytes 651272 | tf_op jit(solution)/shard_map/ppermute | solution.py:724
  9.8 18.6 %collective-permute-start.11 = (f32[496,128]{1,0:T(8,128)}, f32[496,128]{1,0:T(8,128)S(1)}, u32[]{:S(2)}, u32[]{:S(2)}) collective-permute-start(f32[496,128]{1,0:T(8,128)} %get-tuple-element.367), channel_id=1, source_target_pairs={{0,1},{1,2},{2,3},{3,4},{4,5},{5,6},{6,7},{7,0},{8,9},{9,10},{10,1... | collective-permute-start | bytes 761864 | tf_op jit(solution)/shard_map/ppermute | solution.py:724
  9.8 18.6 %collective-permute-start.12 = (f32[496,128]{1,0:T(8,128)}, f32[496,128]{1,0:T(8,128)S(1)}, u32[]{:S(2)}, u32[]{:S(2)}) collective-permute-start(f32[496,128]{1,0:T(8,128)} %get-tuple-element.368), channel_id=1, source_target_pairs={{0,7},{1,0},{2,1},{3,2},{4,3},{5,4},{6,5},{7,6},{8,15},{9,8},{10,9... | collective-permute-start | bytes 761864 | tf_op jit(solution)/shard_map/ppermute | solution.py:724
  13.4 8.2 %collective-permute-start.15 = (f32[72,128]{1,0:T(8,128)}, f32[72,128]{1,0:T(8,128)S(1)}, u32[]{:S(2)}, u32[]{:S(2)}) collective-permute-start(f32[72,128]{1,0:T(8,128)} %get-tuple-element.371), channel_id=1, source_target_pairs={{0,5},{1,6},{2,7},{3,0},{4,1},{5,2},{6,3},{7,4},{8,13},{9,14},{10,... | collective-permute-start | bytes 110600 | tf_op jit(solution)/shard_map/ppermute | solution.py:724
  17.4 0.7 copy-start.15
  17.4 22.7 %copy-start.16 = (f32[6]{0:T(128)S(1)}, f32[6]{0:T(128)}, u32[]{:S(2)}) copy-start(f32[6]{0:T(128)} %refs_14_.1) | copy-start | bytes 76
  17.5 22.7 %copy-start.17 = (f32[2]{0:T(128)S(1)}, f32[2]{0:T(128)}, u32[]{:S(2)}) copy-start(f32[2]{0:T(128)} %refs_15_.1) | copy-start | bytes 28
  17.5 22.7 %copy-start.18 = (s32[2]{0:T(128)S(1)}, s32[2]{0:T(128)}, u32[]{:S(2)}) copy-start(s32[2]{0:T(128)} %refs_16_.1) | copy-start | bytes 28
  17.5 11.0 %collective-permute-start.13 = (f32[424,128]{1,0:T(8,128)S(1)}, f32[424,128]{1,0:T(8,128)S(1)}, u32[]{:S(2)}, u32[]{:S(2)}) collective-permute-start(f32[424,128]{1,0:T(8,128)S(1)} %copy-done.19), channel_id=1, source_target_pairs={{0,2},{1,3},{2,4},{3,5},{4,6},{5,7},{6,0},{7,1},{8,10},{9,11},{10,... | collective-permute-start | bytes 651272 | tf_op jit(solution)/shard_map/ppermute | solution.py:724
  21.6 7.2 %copy-start.1 = (f32[72,128]{1,0:T(8,128)}, f32[72,128]{1,0:T(8,128)S(1)}, u32[]{:S(2)}) copy-start(f32[72,128]{1,0:T(8,128)S(1)} %collective-permute-done.15.refs_4_.refs_10_) | copy-start | bytes 110596
  21.6 6.9 %collective-permute-start.17 = (f32[360,128]{1,0:T(8,128)S(1)}, f32[360,128]{1,0:T(8,128)S(1)}, u32[]{:S(2)}, u32[]{:S(2)}) collective-permute-start(f32[360,128]{1,0:T(8,128)S(1)} %copy-done.20), channel_id=1, source_target_pairs={{0,8},{8,16},{16,24},{24,0},{1,9},{9,17},{17,25},{25,1},{2,10},{10... | collective-permute-start | bytes 552968 | tf_op jit(solution)/shard_map/ppermute | solution.py:724
  24.0 4.9 %copy-start.11 = (f32[424,128]{1,0:T(8,128)}, f32[424,128]{1,0:T(8,128)S(1)}, u32[]{:S(2)}) copy-start(f32[424,128]{1,0:T(8,128)S(1)} %collective-permute-done.14.refs_2_.refs_8_) | copy-start | bytes 651268
  24.0 4.4 %collective-permute-start.16 = (f32[72,128]{1,0:T(8,128)S(1)}, f32[72,128]{1,0:T(8,128)S(1)}, u32[]{:S(2)}, u32[]{:S(2)}) collective-permute-start(f32[72,128]{1,0:T(8,128)S(1)} %copy-done.21), channel_id=1, source_target_pairs={{0,3},{1,4},{2,5},{3,6},{4,7},{5,0},{6,1},{7,2},{8,11},{9,12},{10,... | collective-permute-start | bytes 110600 | tf_op jit(solution)/shard_map/ppermute | solution.py:724
  28.4 11.7 %copy-start.2 = (f32[72,128]{1,0:T(8,128)}, f32[72,128]{1,0:T(8,128)S(1)}, u32[]{:S(2)}) copy-start(f32[72,128]{1,0:T(8,128)S(1)} %collective-permute-done.16.refs_5_.refs_11_) | copy-start | bytes 110596
  28.4 3.4 %copy-start.9 = (f32[496,128]{1,0:T(8,128)}, f32[496,128]{1,0:T(8,128)S(1)}, u32[]{:S(2)}) copy-start(f32[496,128]{1,0:T(8,128)S(1)} %collective-permute-done.11.refs_1_.refs_7_) | copy-start | bytes 761860
  28.4 11.7 %copy-start.10 = (f32[496,128]{1,0:T(8,128)}, f32[496,128]{1,0:T(8,128)S(1)}, u32[]{:S(2)}) copy-start(f32[496,128]{1,0:T(8,128)S(1)} %collective-permute-done.12.refs_0_.refs_6_) | copy-start | bytes 761860
  28.4 11.7 %copy-start = (f32[360,128]{1,0:T(8,128)}, f32[360,128]{1,0:T(8,128)S(1)}, u32[]{:S(2)}) copy-start(f32[360,128]{1,0:T(8,128)S(1)} %collective-permute-done.17.refs_6_.refs_3_) | copy-start | bytes 552964
  28.4 3.4 %copy-start.12 = (f32[424,128]{1,0:T(8,128)}, f32[424,128]{1,0:T(8,128)S(1)}, u32[]{:S(2)}) copy-start(f32[424,128]{1,0:T(8,128)S(1)} %collective-permute-done.13.refs_3_.refs_9_) | copy-start | bytes 651268
  28.8 9.1 %collective-permute-start.18 = (f32[416,128]{1,0:T(8,128)S(1)}, f32[416,128]{1,0:T(8,128)S(1)}, u32[]{:S(2)}, u32[]{:S(2)}) collective-permute-start(f32[416,128]{1,0:T(8,128)S(1)} %get-tuple-element.376), channel_id=1, source_target_pairs={{0,24},{8,0},{16,8},{24,16},{1,25},{9,1},{17,9},{25,17},{2,26},{10... | collective-permute-start | bytes 638984 | tf_op jit(solution)/shard_map/ppermute | solution.py:724
  29.9 10.2 %collective-permute-start.19 = (f32[416,128]{1,0:T(8,128)S(1)}, f32[416,128]{1,0:T(8,128)}, u32[]{:S(2)}, u32[]{:S(2)}) collective-permute-start(f32[416,128]{1,0:T(8,128)S(1)} %get-tuple-element.377), channel_id=1, source_target_pairs={{0,8},{8,16},{16,24},{24,0},{1,9},{9,17},{17,25},{25,1},{2,10},{10... | collective-permute-start | bytes 638984 | tf_op jit(solution)/shard_map/ppermute | solution.py:724
  38.0 2.1 %copy-start.13 = (f32[416,128]{1,0:T(8,128)}, f32[416,128]{1,0:T(8,128)S(1)}, u32[]{:S(2)}) copy-start(f32[416,128]{1,0:T(8,128)S(1)} %collective-permute-done.18.refs_4_) | copy-start | bytes 638980
  58.7 13.3 %collective-permute-start.4 = (f32[7,128,128]{2,1,0:T(8,128)}, f32[7,128,128]{2,1,0:T(8,128)S(1)}, u32[]{:S(2)}, u32[]{:S(2)}) collective-permute-start(f32[7,128,128]{2,1,0:T(8,128)} %get-tuple-element.284), channel_id=1, source_target_pairs={{0,4},{1,5},{2,6},{3,7},{4,0},{5,1},{6,2},{7,3},{8,12},{9,13},{10,... | collective-permute-start | bytes 1376264 | tf_op jit(solution)/shard_map/cond/branch_3_fun/ppermute | solution.py:885
  60.5 20.8 %copy-start.6 = (f32[7,128,128]{2,1,0:T(8,128)S(1)}, f32[7,128,128]{2,1,0:T(8,128)}, u32[]{:S(2)}) copy-start(f32[7,128,128]{2,1,0:T(8,128)} %get-tuple-element.268.refs_0_) | copy-start | bytes 1376260 | tf_op jit(solution)/shard_map/cond
  67.7 13.7 %collective-permute-start.5 = (f32[7,128,128]{2,1,0:T(8,128)S(1)}, f32[7,128,128]{2,1,0:T(8,128)S(1)}, u32[]{:S(2)}, u32[]{:S(2)}) collective-permute-start(f32[7,128,128]{2,1,0:T(8,128)S(1)} %get-tuple-element.285), channel_id=1, source_target_pairs={{0,4},{1,5},{2,6},{3,7},{4,0},{5,1},{6,2},{7,3},{8,12},{9,13},{10,... | collective-permute-start | bytes 1376264 | tf_op jit(solution)/shard_map/cond/branch_3_fun/ppermute | solution.py:885
